TPU v7x, 512 devices: a whole 4x8x8 slice. The times are simulated.
512 devices in a mesh: island: 16 (over y_hi, x), expert: 32 (over z, y_lo, core).
Axes of the slice: x: 4, y: 8 (y_hi: 4, y_lo: 2; y = y_hi * 2 + y_lo), z: 8, core: 2. Of those that a mesh axis runs over, the one named last changes fastest.
Arguments:
- tokens: bfloat16 [1, 65536, 5120], P(None, ('island', 'expert')), may hold values from -6 to 6
- targets: bfloat16 [1, 65536, 5120], P(None, ('island', 'expert')), may hold values from -6 to 6
- expert_ids: int32 [1, 65536, 6], P(None, ('island', 'expert')), may hold values from 0 to 159, as said below
- gate_weights: float32 [1, 65536, 6], P(None, ('island', 'expert')), may hold values from 0.1 to 1
- gate_proj: bfloat16 [3072, 5120], P('expert', 'island'), may hold values from -0.078125 to 0.078125
- up_proj: bfloat16 [3072, 5120], P('expert', 'island'), may hold values from -0.078125 to 0.078125
- down_global: float32 [3072, 5120], P('expert', 'island'), may hold values from -0.21875 to 0.21875
- outer_momentum: float32 [3072, 5120], P('expert', 'island'), may hold values from -0.003 to 0.003
- inner_first: bfloat16 [16, 3072, 5120], P('island', 'expert'), may hold values from -1.1953125 to 1.1953125
- inner_second: bfloat16 [16, 3072, 5120], P('island', 'expert'), may hold values from 0.5 to 8
Outputs:
- new_down: float32 [3072, 5120], P('expert', 'island')
- new_momentum: float32 [3072, 5120], P('expert', 'island')
Inputs may be any that keep to these rules, and one draw needn't show every extreme that they name: `expert_ids`: A row's 6 ids are different. In each inner step and each aligned block of 128 rows (the rows of one device), a row names at most one id below 4, each id below 4 is named by at most 8 rows, and in every block one of them is named by exactly 8 rows.
All inputs are finite; a program needn't handle non-finite values.
Results may differ from a plain program's by a relative error of at most 0.0051.
Values may be sent and summed in bfloat16 or wider, within the bound.
A program may use at most 64 MiB of HBM per device.

v0:
```python
import jax
import jax.numpy as jnp
from jax import lax
from jax.sharding import PartitionSpec as P

GROUP = 8
CAP = 8


beta_first = 0.9
beta_second = 0.95
inner_rate = 0.01
decay_rate = 0.1
epsilon = 1e-08
outer_rate = 0.7
outer_mu = 0.9


def route_table(expert_ids, gate_weights, window):
    hit = expert_ids < window
    chosen = jnp.sum(jnp.where(hit, expert_ids, 0), axis=1)
    routed = jnp.any(hit, axis=1)
    weight = jnp.sum(jnp.where(hit, gate_weights, jnp.zeros_like(gate_weights)), axis=1)
    member = (chosen[:, None] == jnp.arange(window, dtype=jnp.int32)[None, :]) & routed[:, None]
    rank = jnp.cumsum(member.astype(jnp.int32), axis=0) - 1
    places = member[:, :, None] & (
        rank[:, :, None] == jnp.arange(CAP, dtype=jnp.int32)[None, None, :]
    )
    select = places.reshape(expert_ids.shape[0], window * CAP).T.astype(jnp.float32)
    return (select, weight)


def outbound(select, values, window):
    picked = jnp.dot(select.astype(jnp.bfloat16), values, preferred_element_type=jnp.float32)
    return jnp.repeat(picked.astype(jnp.bfloat16).reshape(window, CAP, -1), GROUP, axis=0)


def on_device(
    tokens,
    targets,
    expert_ids,
    gate_weights,
    gate_proj,
    up_proj,
    down_global,
    outer_momentum,
    inner_first,
    inner_second,
):
    devices = lax.axis_size("expert")
    window = devices // GROUP
    islands = lax.axis_size("island")
    width = tokens.shape[2]
    weights = lax.all_gather(down_global, "island", axis=1, tiled=True)
    gate_full, up_full = (
        lax.all_gather(gate_proj, "island", axis=1, tiled=True),
        lax.all_gather(up_proj, "island", axis=1, tiled=True),
    )
    start_weights = weights
    first = inner_first[0].astype(jnp.float32)
    second = inner_second[0].astype(jnp.float32)
    select, weight = route_table(expert_ids[0], gate_weights[0], window)
    rows = lax.all_to_all(
        outbound(select, tokens[0], window), "expert", split_axis=0, concat_axis=0, tiled=True
    ).reshape(-1, width)
    pre_gate = jnp.einsum("rd,hd->rh", rows, gate_full, preferred_element_type=jnp.float32)
    pre_up = jnp.einsum("rd,hd->rh", rows, up_full, preferred_element_type=jnp.float32)
    active = (jax.nn.silu(pre_gate) * pre_up).astype(jnp.bfloat16)
    partial_value = jnp.dot(
        active, weights.astype(jnp.bfloat16), preferred_element_type=jnp.float32
    )
    partial_value = partial_value.reshape(devices, CAP, width)
    returned = lax.all_to_all(partial_value, "expert", split_axis=0, concat_axis=0, tiled=True)
    output = jnp.sum(returned.reshape(window, GROUP, CAP, width), axis=1)
    aims = jnp.dot(
        select.astype(jnp.bfloat16), targets[0], preferred_element_type=jnp.float32
    ).reshape(window, CAP, width)
    scales = jnp.dot(select, weight, precision=lax.Precision.HIGHEST).reshape(window, CAP, 1)
    errors = (scales * (scales * output - aims)).astype(jnp.bfloat16)
    landed = lax.all_to_all(
        jnp.repeat(errors, GROUP, axis=0), "expert", split_axis=0, concat_axis=0, tiled=True
    ).reshape(-1, width)
    grads = jnp.einsum("rh,rd->hd", active, landed, preferred_element_type=jnp.float32)
    first = beta_first * first + (1.0 - beta_first) * grads
    second = beta_second * second + (1.0 - beta_second) * grads * grads
    weights = weights - inner_rate * (first / (jnp.sqrt(second) + epsilon) + decay_rate * weights)
    delta = start_weights - weights
    columns = down_global.shape[1]
    total = lax.psum(delta, "island")
    mine = lax.dynamic_slice_in_dim(total, lax.axis_index("island") * columns, columns, 1)
    mean = mine / islands
    new_momentum = outer_mu * outer_momentum + mean
    new_down = down_global - outer_rate * (mean + outer_mu * new_momentum)
    return (new_down, new_momentum)


def solution(mesh):
    return jax.shard_map(
        on_device,
        mesh=mesh,
        in_specs=(
            P(None, ("island", "expert"), None),
            P(None, ("island", "expert"), None),
            P(None, ("island", "expert"), None),
            P(None, ("island", "expert"), None),
            P("expert", "island"),
            P("expert", "island"),
            P("expert", "island"),
            P("expert", "island"),
            P("island", "expert", None),
            P("island", "expert", None),
        ),
        out_specs=(P("expert", "island"), P("expert", "island")),
        check_vma=False,
    )
```

profile of v0, /device:TPU:1, one launch (start us, length us, event | category | flops | bytes accessed | tf_op | source)
XLA Modules:
  0.0 593.5 jit_solution(15182148449212197622)
XLA Ops:
  7.2 0.8 fusion.42
  8.0 0.7 fusion.44
  9.2 0.4 fusion.2
  9.6 1.8 broadcast_in_dim.20
  11.4 13.2 %all-to-all-start = ((bf16[32,8,5120]{2,1,0:T(8,128)(2,1)}), bf16[32,8,5120]{2,1,0:T(8,128)(2,1)}, u32[]{:S(2)}, u32[]{:S(2)}) async-start(bf16[32,8,5120]{2,1,0:T(8,128)(2,1)} %bitcast.127), calls=%async_computation | async-start | bytes 5242880 | tf_op jit(solution)/shard_map/all_to_all | solution.py:63
  24.6 0.7 all-gather.5.cloned.1.call-update
  25.3 96.6 %all-gather.1 = bf16[16,320,96]{1,2,0:T(8,128)(2,1)S(1)} all-gather(bf16[1,320,96]{1,2,0:T(8,128)(2,1)S(1)} %bitcast.130), channel_id=1, replica_groups=mesh['island'=16,'expert'=32] {'island'}, dimensions={0}, use_global_device_ids=true | all-gather | bytes 1044480 | tf_op jit(solution)/shard_map/all_gather | solution.py:56
  122.0 0.4 copy.23
  122.4 1.7 reshape.129
  124.1 40.0 %all-gather.2 = bf16[16,320,96]{1,2,0:T(8,128)(2,1)S(1)} all-gather(bf16[1,320,96]{1,2,0:T(8,128)(2,1)S(1)} %bitcast.131), channel_id=1, replica_groups=mesh['island'=16,'expert'=32] {'island'}, dimensions={0}, use_global_device_ids=true | all-gather | bytes 1044480 | tf_op jit(solution)/shard_map/all_gather | solution.py:57
  164.1 0.4 copy.24
  164.5 1.8 reshape.131
  166.3 4.5 copy.20
  170.8 2.0 reshape.127
  172.8 3.0 fusion.7
  175.9 2.7 fusion.22
  178.6 3.2 convolution_bitcast_fusion
  181.8 35.3 %all-to-all-start.1 = ((f32[32,8,5120]{2,1,0:T(8,128)}), f32[32,8,5120]{2,1,0:T(8,128)}, u32[]{:S(2)}, u32[]{:S(2)}) async-start(f32[32,8,5120]{2,1,0:T(8,128)} %convolution_bitcast_fusion), calls=%async_computation.1 | async-start | bytes 10485760 | tf_op jit(solution)/shard_map/all_to_all | solution.py:73
  217.4 122.3 %all-to-all-done.1 = f32[32,8,5120]{2,1,0:T(8,128)} async-done(((f32[32,8,5120]{2,1,0:T(8,128)}), f32[32,8,5120]{2,1,0:T(8,128)}, u32[]{:S(2)}, u32[]{:S(2)}) %all-to-all-start.1) | async-done | bytes 5242912 | tf_op jit(solution)/shard_map/all_to_all | solution.py:73
  339.8 2.9 bitcast_reduce_fusion
  343.4 74.1 %all_to_all.15 = bf16[32,8,5120]{2,1,0:T(8,128)(2,1)S(1)} all-to-all(bf16[32,8,5120]{2,1,0:T(8,128)(2,1)S(1)} %bitcast.128), channel_id=1, replica_groups=mesh['island'=16,'expert'=32] {'expert'}, dimensions={0} | all-to-all | bytes 5242880 | tf_op jit(solution)/shard_map/all_to_all | solution.py:80
  417.5 3.2 subtract_subtract_fusion
  420.6 164.2 %all-reduce.2.cloned.1.call-done = f32[96,5120]{1,0:T(8,128)} async-done(((f32[96,5120]{1,0:T(8,128)}), f32[96,5120]{1,0:T(8,128)}) %all-reduce.2.cloned.1.call-update) | async-done | bytes 1966096 | tf_op jit(solution)/shard_map/psum | solution.py:89
  584.9 1.7 multiply_subtract_fusion
  (38 shorter events, 1.6 us)
Async XLA Ops:
  7.2 2.1 copy-start
  11.4 13.9 %copy-start.5 = (bf16[96,320]{1,0:T(8,128)(2,1)S(1)}, bf16[96,320]{1,0:T(8,128)(2,1)}, u32[]{:S(2)}) copy-start(bf16[96,320]{1,0:T(8,128)(2,1)} %param.14) | copy-start | bytes 184324
  11.4 161.4 %all-to-all-start = ((bf16[32,8,5120]{2,1,0:T(8,128)(2,1)}), bf16[32,8,5120]{2,1,0:T(8,128)(2,1)}, u32[]{:S(2)}, u32[]{:S(2)}) async-start(bf16[32,8,5120]{2,1,0:T(8,128)(2,1)} %bitcast.127), calls=%async_computation | async-start | bytes 5242880 | tf_op jit(solution)/shard_map/all_to_all | solution.py:63
  24.6 141.7 %all-gather.5.cloned.1.call-start = ((), (), s32[]{:S(2)}) async-start(), calls=%async_computation.4 | async-start | bytes 2506752 | tf_op jit(solution)/shard_map/all_gather | solution.py:54
  122.0 2.1 copy-start.6
  172.8 3.0 copy-start.1
  181.8 35.3 %copy-start.7 = (s32[1,128,6]{1,0,2:T(1,128)S(1)}, s32[1,128,6]{1,0,2:T(1,128)}, u32[]{:S(2)}) copy-start(s32[1,128,6]{1,0,2:T(1,128)} %param.12) | copy-start | bytes 9220
  181.8 35.4 %copy-start.8 = (f32[1,128,6]{1,0,2:T(1,128)S(1)}, f32[1,128,6]{1,0,2:T(1,128)}, u32[]{:S(2)}) copy-start(f32[1,128,6]{1,0,2:T(1,128)} %param.13) | copy-start | bytes 9220
  181.8 158.0 %all-to-all-start.1 = ((f32[32,8,5120]{2,1,0:T(8,128)}), f32[32,8,5120]{2,1,0:T(8,128)}, u32[]{:S(2)}, u32[]{:S(2)}) async-start(f32[32,8,5120]{2,1,0:T(8,128)} %convolution_bitcast_fusion), calls=%async_computation.1 | async-start | bytes 10485760 | tf_op jit(solution)/shard_map/all_to_all | solution.py:73
  217.1 367.8 %all-reduce.2.cloned.1.call-start = ((), (), s32[]{:S(2)}) async-start(), calls=%async_computation.3 | async-start | bytes 3932160 | tf_op jit(solution)/shard_map/psum | solution.py:89
  339.8 2.9 copy-start.2
  343.3 74.1 %copy-start.9 = (bf16[1,96,5120]{2,1,0:T(8,128)(2,1)S(1)}, bf16[1,96,5120]{2,1,0:T(8,128)(2,1)}, u32[]{:S(2)}) copy-start(bf16[1,96,5120]{2,1,0:T(8,128)(2,1)} %param.19) | copy-start | bytes 2949124
  343.3 74.1 %copy-start.10 = (bf16[1,96,5120]{2,1,0:T(8,128)(2,1)S(1)}, bf16[1,96,5120]{2,1,0:T(8,128)(2,1)}, u32[]{:S(2)}) copy-start(bf16[1,96,5120]{2,1,0:T(8,128)(2,1)} %param.18) | copy-start | bytes 2949124
  420.6 164.3 %copy-start.3 = (f32[96,320]{1,0:T(8,128)S(1)}, f32[96,320]{1,0:T(8,128)}, u32[]{:S(2)}) copy-start(f32[96,320]{1,0:T(8,128)} %param.16) | copy-start | bytes 368644
  420.6 164.3 %copy-start.4 = (f32[96,320]{1,0:T(8,128)S(1)}, f32[96,320]{1,0:T(8,128)}, u32[]{:S(2)}) copy-start(f32[96,320]{1,0:T(8,128)} %param.17) | copy-start | bytes 368644
Sparse Core Ops, SparseCore 0:
  28.4 74.1 all-gather.4
  420.8 164.0 all-reduce.1
where the time goes:
time: 603 us; the launch traced here: 593 us
  waiting for transfers between devices  287 us (48%)
  blocking collectives  211 us (35%)
  starting transfers between devices  48.5 us (8%)
  between operations  14.2 us (2%)
  local copies, waits for them, and re-layouts  13.2 us (2%)
  matrix products  13.1 us (2%)
  other arithmetic  6.46 us (1%)
    psum x1, waiting for transfers between devices, on_device(): total = lax.psum(delta, 'island')  164 us
    all_to_all x1, waiting for transfers between devices, on_device(): lax.all_to_all(partial_value, 'expert', split_axis=0, concat_axis=0, tile...  122 us
    all_gather x1, blocking collectives, on_device(): lax.all_gather(gate_proj, 'island', axis=1, tiled=True)  96.6 us
    all_to_all x1, blocking collectives, on_device(): lax.all_to_all(jnp.repeat(errors, GROUP, axis=0), 'expert', split_axis=0,...  74.1 us
    all_gather x1, blocking collectives, on_device(): lax.all_gather(up_proj, 'island', axis=1, tiled=True)  40 us
    all_to_all x1, starting transfers between devices, on_device(): lax.all_to_all(partial_value, 'expert', split_axis=0, concat_axis=0, tile...  35.3 us
    all_to_all x1, starting transfers between devices, on_device(): lax.all_to_all(outbound(select, tokens[0], window), 'expert', split_axis=...  13.2 us
  transfers between devices with their start and end apart: 4, of which 2 were waited for; matrix products, arithmetic and copies ran while one was open for 2% of the time, Pallas kernels for 0%

commit v1 on v0

v1 whole, which is shorter than its diff:
```python
import jax
import jax.numpy as jnp
from jax import lax
from jax.experimental import pallas as pl
from jax.experimental.pallas import tpu as pltpu
from jax.sharding import PartitionSpec as P

CAP = 8
SLOT = 2 * CAP
LANES = 128

beta_first = 0.9
beta_second = 0.95
inner_rate = 0.01
decay_rate = 0.1
epsilon = 1e-08
outer_rate = 0.7
outer_mu = 0.9

F32 = jnp.float32
BF16 = jnp.bfloat16
MESH = pl.DeviceIdType.MESH
ROWS_T = (((0,), (0,)), ((), ()))
COLS_T = (((1,), (1,)), ((), ()))


def wait_for(ref, sem):
    pltpu.make_async_copy(ref, ref, sem).wait()


def loop(low, high, body):
    lax.fori_loop(low, high, lambda i, _: (body(i), 0)[1], 0)


def kernel(
    tok_hbm, tgt_hbm, ids_ref, gw_ref, gate_ref, up_ref, down_ref, m_hbm, v_hbm,
    out_ref,
    tok, tgt, sel, sbuf, xyb, xs, xp, ys, gs, lhs,
    gut, dt, gu, dd, dx, mv, part, pr, ab, wn, eb, gr, ub, r1, st, r2,
    in_sem, gu_s, gu_r, gus1_s, d_s, d_r, ds1_s, xy_s, xy_r, xp_s, xp_r, dx_s, dx_r,
    mv_s, mv_r, p_s, p_r, a_s, a_r, u_s, u_r, t_s, t_r,
):
    isl = lax.axis_index("island")
    t = lax.axis_index("expert")
    x, yh = lax.rem(isl, 4), lax.div(isl, 4)
    e, pos = lax.div(t, 8), lax.rem(t, 8)
    c, core = lax.div(pos, 2), lax.rem(pos, 2)
    base = 8 * e
    pair = t + 1 - 2 * core
    right = yh * 4 + lax.rem(x + 1, 4)
    left = yh * 4 + lax.rem(x + 3, 4)
    hid, chunk = gate_ref.shape
    half = hid // 2
    cw = 2 * chunk
    home = c == yh
    away = c != yh

    def send(src, dst, s, r, island, expert):
        pltpu.make_async_remote_copy(
            src_ref=src, dst_ref=dst, send_sem=s, recv_sem=r,
            device_id=(island, expert), device_id_type=MESH,
        ).start()

    barrier = pltpu.get_barrier_semaphore()

    def tell(island, expert):
        pl.semaphore_signal(barrier, inc=1, device_id=(island, expert), device_id_type=MESH)

    loop(1, 32, lambda i: tell(isl, lax.rem(t + i, 32)))
    for d in range(1, 4):
        for k in range(2):
            tell(yh * 4 + lax.rem(x + d, 4), base + 2 * c + k)
        tell(lax.rem(yh + d, 4) * 4 + x, base + 2 * yh + core)

    @pl.when(away)
    def _():
        for q in range(4):
            tell(c * 4 + x, base + 2 * q + core)

    load_tok = pltpu.make_async_copy(tok_hbm, tok, in_sem.at[0])
    load_tgt = pltpu.make_async_copy(tgt_hbm, tgt, in_sem.at[1])
    load_tok.start()
    load_tgt.start()

    row = lax.broadcasted_iota(jnp.int32, (chunk, cw), 0)
    col = lax.broadcasted_iota(jnp.int32, (chunk, cw), 1)
    put0 = (col == row).astype(F32).astype(BF16)
    put1 = (col == row + chunk).astype(F32).astype(BF16)

    def dot(a, b):
        return jnp.dot(a, b, preferred_element_type=F32)

    gut[...] = (dot(gate_ref[...], put0) + dot(up_ref[...], put1)).astype(BF16)
    down = down_ref[...].astype(BF16)
    dt[...] = (dot(down[:half], put0) + dot(down[half:], put1)).astype(BF16)

    n_tok = ids_ref.shape[0]
    lane = lax.broadcasted_iota(jnp.int32, (n_tok, 4 * SLOT), 1)
    named = lax.div(lane, SLOT)
    ids = ids_ref[...]
    member = jnp.zeros((n_tok, 4 * SLOT), F32)
    for j in range(ids.shape[1]):
        member = member + (ids[:, j:j + 1] == named).astype(F32)
    before = (
        lax.broadcasted_iota(jnp.int32, (n_tok, n_tok), 1)
        < lax.broadcasted_iota(jnp.int32, (n_tok, n_tok), 0)
    ).astype(F32).astype(BF16)
    rank = dot(before, member.astype(BF16))
    picked = jnp.where(rank == lax.rem(lane, CAP).astype(F32), member, 0.0)
    of_x = lax.rem(lane, SLOT) < CAP
    same = (
        lax.broadcasted_iota(jnp.int32, (n_tok, n_tok), 1)
        == lax.broadcasted_iota(jnp.int32, (n_tok, n_tok), 0)
    ).astype(F32).astype(BF16)
    for j, part_of in enumerate((of_x, jnp.logical_not(of_x))):
        chosen = jnp.where(part_of, picked, 0.0).astype(BF16)
        sel[j] = lax.dot_general(chosen, same, ROWS_T, preferred_element_type=F32).astype(BF16)
    weight = jnp.sum(jnp.where(ids < 4, gw_ref[...], 0.0), axis=1, keepdims=True)
    high = weight.astype(BF16)
    rest = weight - high.astype(F32)
    mid = rest.astype(BF16)
    low = (rest - mid.astype(F32)).astype(BF16)
    glane = lax.broadcasted_iota(jnp.int32, (n_tok, LANES), 1)
    gmat = jnp.where(glane == 0, high.astype(F32), 0.0)
    gmat = jnp.where(glane == 1, mid.astype(F32), gmat)
    gmat = jnp.where(glane == 2, low.astype(F32), gmat)
    gates = dot(sel[0], gmat.astype(BF16)).astype(BF16)

    pl.semaphore_wait(barrier, jnp.where(away, 44, 40))

    def first_stage(tile, buf, s, r):
        for d in range(1, 4):
            send(tile, buf.at[0, c], s, r.at[0, c], lax.rem(yh + d, 4) * 4 + x, base + 2 * yh + core)

        @pl.when(away)
        def _():
            send(tile, buf.at[0, c], s, r.at[0, c], isl, base + 2 * yh + core)

        @pl.when(home)
        def _():
            pltpu.make_async_copy(tile, buf.at[0, c], r.at[0, c]).start()

    first_stage(gut, gu, gus1_s, gu_r)

    load_tok.wait()
    load_tgt.wait()

    def dispatch(p):
        cols = pl.ds(pl.multiple_of(p * cw, LANES), cw)
        sbuf[p, :, 0:cw] = (dot(sel[0], tok[:, cols]) + dot(sel[1], tgt[:, cols])).astype(BF16)
        sbuf[p, :, cw:cw + LANES] = gates
        for j in range(4):
            block = sbuf.at[p, pl.ds(j * SLOT, SLOT)]

            @pl.when(8 * j + p != t)
            def _():
                send(block, xyb.at[t], xy_s, xy_r, isl, 8 * j + p)

            @pl.when(8 * j + p == t)
            def _():
                pltpu.make_async_copy(block, xyb.at[t], xy_r).start()

    loop(0, 8, dispatch)
    first_stage(dt, dd, ds1_s, d_r)

    def moments(p):
        cols = pl.ds(pl.multiple_of(p * cw, LANES), cw)
        for j, ref in enumerate((m_hbm, v_hbm)):

            @pl.when(p != pos)
            def _():
                send(ref.at[:, cols], mv.at[j, pos], mv_s, mv_r, isl, base + p)

            @pl.when(p == pos)
            def _():
                pltpu.make_async_copy(ref.at[:, cols], mv.at[j, pos], mv_r).start()

    me = base + pos

    def around(buf, s, r):
        def body(q):
            wait_for(buf.at[0, q], r.at[0, q])
            send(buf.at[0, q], buf.at[3, q], s, r.at[3, q], right, me)
            send(buf.at[0, q], buf.at[1, q], s, r.at[1, q], left, me)

        loop(0, 4, body)

    def forward(buf, s, r):
        def body(q):
            wait_for(buf.at[3, q], r.at[3, q])
            send(buf.at[3, q], buf.at[2, q], s, r.at[2, q], right, me)
            wait_for(buf.at[1, q + 2], r.at[1, q + 2])
            send(buf.at[1, q + 2], buf.at[2, q + 2], s, r.at[2, q + 2], left, me)

        loop(0, 2, body)

    def others(buf, r):
        def body(q):
            wait_for(buf.at[3, q + 2], r.at[3, q + 2])
            wait_for(buf.at[1, q], r.at[1, q])

        loop(0, 2, body)

    def far(buf, r):
        loop(0, 4, lambda q: wait_for(buf.at[2, q], r.at[2, q]))

    around(gu, gu_s, gu_r)
    loop(0, 8, moments)

    in_low = lax.broadcasted_iota(jnp.int32, (8 * CAP, cw), 1) < chunk

    def spread(v, h, rows):
        turned = pltpu.roll(v, chunk, 1)
        up_rows = pl.ds(rows.start + 32 * CAP, rows.size)
        lhs[2 * h, rows] = jnp.where(in_low, v, 0.0).astype(BF16)
        lhs[2 * h, up_rows] = jnp.where(in_low, 0.0, turned).astype(BF16)
        lhs[2 * h + 1, rows] = jnp.where(in_low, turned, 0.0).astype(BF16)
        lhs[2 * h + 1, up_rows] = jnp.where(in_low, 0.0, v).astype(BF16)

    wait_for(xyb, xy_r)

    def unpack(i):
        v = xyb[pl.ds(8 * i, 8)].astype(F32)
        rows = pl.ds(pl.multiple_of(i * 8 * CAP, 8 * CAP), 8 * CAP)
        xv = v[:, :CAP, :cw].reshape(8 * CAP, cw)
        xs[rows] = xv.astype(BF16)
        ys[rows] = v[:, CAP:, :cw].reshape(8 * CAP, cw)
        total = jnp.sum(v[:, :CAP, cw:].reshape(8 * CAP, LANES), axis=1, keepdims=True)
        gs[rows] = jnp.broadcast_to(total, (8 * CAP, LANES))
        spread(xv, core, rows)

    loop(0, 4, unpack)
    send(xs, xp, xp_s, xp_r, isl, pair)
    forward(gu, gu_s, gu_r)
    around(dd, d_s, d_r)
    wait_for(xp, xp_r)

    def unpack_pair(i):
        rows = pl.ds(pl.multiple_of(i * 8 * CAP, 8 * CAP), 8 * CAP)
        spread(xp[rows].astype(F32), 1 - core, rows)

    loop(0, 4, unpack_pair)

    def pre(rel):
        made = lax.dot_general(
            lhs[lax.rem(x + rel, 4)], gu[rel].reshape(4 * hid, cw), COLS_T, preferred_element_type=F32
        )
        return made.reshape(2, 4, 8 * CAP, 4 * hid)

    part[...] = pre(0)
    others(gu, gu_r)
    part[...] += pre(1)
    part[...] += pre(3)
    far(gu, gu_r)
    part[...] += pre(2)
    for d in range(1, 4):
        q = lax.rem(c + d, 4)
        send(part.at[:, q], pr.at[4 - d], p_s, p_r.at[4 - d], isl, base + 2 * q + core)
    forward(dd, d_s, d_r)
    for d in range(1, 4):
        wait_for(pr.at[d], p_r.at[d])
    gate_sum = part[0, c] + pr[1, 0] + pr[2, 0] + pr[3, 0]
    up_sum = part[1, c] + pr[1, 1] + pr[2, 1] + pr[3, 1]
    mine = 4 * core + c
    ab[mine] = (gate_sum * jax.nn.sigmoid(gate_sum) * up_sum).astype(BF16)
    loop(1, 8, lambda i: send(ab.at[mine], ab.at[mine], a_s, a_r, isl, base + lax.rem(pos + i, 8)))

    others(dd, d_r)
    far(dd, d_r)
    for j in range(2):
        rel = lax.rem(2 * (1 - core) + j + 4 - x, 4)
        send(dd.at[rel], dx.at[j], dx_s, dx_r.at[j], isl, pair)
    in_low_h = lax.broadcasted_iota(jnp.int32, (half, cw), 1) < chunk

    def lay(k, q, w0, w1):
        top = pl.multiple_of(q * hid, hid)
        w0, w1 = w0.astype(F32), w1.astype(F32)
        wn[k, pl.ds(top, half)] = jnp.where(in_low_h, w0, pltpu.roll(w1, chunk, 1)).astype(BF16)
        wn[k, pl.ds(top + half, half)] = jnp.where(in_low_h, pltpu.roll(w0, chunk, 1), w1).astype(BF16)

    rel0 = lax.rem(2 * core + 4 - x, 4)
    rel1 = lax.rem(2 * core + 5 - x, 4)
    loop(0, 4, lambda q: lay(core, q, dd[rel0, q], dd[rel1, q]))
    for j in range(2):
        wait_for(dx.at[j], dx_r.at[j])
    loop(0, 4, lambda q: lay(1 - core, q, dx[0, q], dx[1, q]))

    wait_for(ab.at[pl.ds(0, 7)], a_r)

    def acts(k):
        return ab[4 * k:4 * k + 4].reshape(32 * CAP, 4 * hid)

    g = gs[:, 0:1]
    output = dot(acts(0), wn[0]) + dot(acts(1), wn[1])
    eb[...] = (g * (g * output - ys[...])).astype(BF16)
    wait_for(mv, mv_r)
    for k in range(2):
        gr[...] = lax.dot_general(acts(k), eb[...], ROWS_T, preferred_element_type=F32)

        def adam(q):
            grad = gr[pl.ds(pl.multiple_of(q * hid, hid), hid)]
            first = beta_first * mv[0, 2 * q + k].astype(F32) + (1.0 - beta_first) * grad
            second = beta_second * mv[1, 2 * q + k].astype(F32) + (1.0 - beta_second) * grad * grad
            step = first / (jnp.sqrt(second) + epsilon)
            upper, lower = step[:half], step[half:]
            ub[0, k, q] = jnp.where(in_low_h, upper, pltpu.roll(lower, chunk, 1)).astype(BF16)
            ub[1, k, q] = jnp.where(in_low_h, pltpu.roll(upper, chunk, 1), lower).astype(BF16)

        loop(0, 4, adam)
        for j in range(2):
            stays = jnp.logical_and(2 * core + j == x, core == k)

            @pl.when(jnp.logical_not(stays))
            def _():
                send(ub.at[j, k], r1.at[x], u_s.at[j, k], u_r.at[x], yh * 4 + 2 * core + j, base + 2 * c + k)

            @pl.when(stays)
            def _():
                pltpu.make_async_copy(ub.at[j, k], r1.at[x], u_r.at[x]).start()

    loop(0, 4, lambda i: wait_for(r1.at[i], u_r.at[i]))

    def column(q):
        total = r1[0, q].astype(F32) + r1[1, q].astype(F32) + r1[2, q].astype(F32) + r1[3, q].astype(F32)
        st[q] = total.astype(st.dtype)
        stays = jnp.logical_and(home, q == c)

        @pl.when(jnp.logical_not(stays))
        def _():
            send(st.at[q], r2.at[yh], t_s.at[q], t_r.at[yh], c * 4 + x, base + 2 * q + core)

        @pl.when(stays)
        def _():
            pltpu.make_async_copy(st.at[q], r2.at[yh], t_r.at[yh]).start()

    loop(0, 4, column)
    loop(0, 4, lambda i: wait_for(r2.at[i], t_r.at[i]))
    out_ref[...] = r2[0].astype(F32) + r2[1].astype(F32) + r2[2].astype(F32) + r2[3].astype(F32)

    for buf, s, s1 in ((gu, gu_s, gus1_s), (dd, d_s, ds1_s)):
        wait_for(buf.at[pl.ds(0, 3)], s)

        @pl.when(away)
        def _():
            wait_for(buf.at[0], s1)

        @pl.when(home)
        def _():
            wait_for(buf.at[0, pl.ds(0, 3)], s1)

    wait_for(xyb.at[pl.ds(0, 31)], xy_s)
    wait_for(xs, xp_s)
    wait_for(dx, dx_s)
    wait_for(mv.at[:, pl.ds(0, 7)], mv_s)
    wait_for(pr.at[pl.ds(0, 3)], p_s)
    wait_for(ab.at[pl.ds(0, 7)], a_s)
    for j in range(2):
        for k in range(2):

            @pl.when(jnp.logical_not(jnp.logical_and(2 * core + j == x, core == k)))
            def _():
                wait_for(ub.at[j, k], u_s.at[j, k])

    def left_st(q):
        @pl.when(jnp.logical_not(jnp.logical_and(home, q == c)))
        def _():
            wait_for(st.at[q], t_s.at[q])

    loop(0, 4, left_st)


def summed_steps(tokens, targets, expert_ids, gate_weights, gate_proj, up_proj, down_global, first, second):
    n_tok, width = tokens.shape
    hid, chunk = gate_proj.shape
    half, cw = hid // 2, 2 * chunk
    rows = 32 * CAP
    dma = pltpu.SemaphoreType.DMA
    anywhere = pl.BlockSpec(memory_space=pl.ANY)
    vmem = pl.BlockSpec(memory_space=pltpu.VMEM)
    scratch = [
        pltpu.VMEM((n_tok, width), BF16),
        pltpu.VMEM((n_tok, width), BF16),
        pltpu.VMEM((2, 4 * SLOT, n_tok), BF16),
        pltpu.VMEM((8, 4 * SLOT, cw + LANES), BF16),
        pltpu.VMEM((32, SLOT, cw + LANES), BF16),
        pltpu.VMEM((rows, cw), BF16),
        pltpu.VMEM((rows, cw), BF16),
        pltpu.VMEM((rows, cw), F32),
        pltpu.VMEM((rows, LANES), F32),
        pltpu.VMEM((4, 2 * rows, cw), BF16),
        pltpu.VMEM((hid, cw), BF16),
        pltpu.VMEM((half, cw), BF16),
        pltpu.VMEM((4, 4, hid, cw), BF16),
        pltpu.VMEM((4, 4, half, cw), BF16),
        pltpu.VMEM((2, 4, half, cw), BF16),
        pltpu.VMEM((2, 8, hid, cw), BF16),
        pltpu.VMEM((2, 4, 8 * CAP, 4 * hid), F32),
        pltpu.VMEM((4, 2, 8 * CAP, 4 * hid), F32),
        pltpu.VMEM((8, 8 * CAP, 4 * hid), BF16),
        pltpu.VMEM((2, 4 * hid, cw), BF16),
        pltpu.VMEM((rows, cw), BF16),
        pltpu.VMEM((4 * hid, cw), F32),
        pltpu.VMEM((2, 2, 4, half, cw), BF16),
        pltpu.VMEM((4, 4, half, cw), BF16),
        pltpu.VMEM((4, half, cw), BF16),
        pltpu.VMEM((4, half, cw), BF16),
        dma((2,)),
        dma, dma((4, 4)), dma,
        dma, dma((4, 4)), dma,
        dma, dma, dma, dma,
        dma, dma((2,)),
        dma, dma,
        dma, dma((4,)),
        dma, dma,
        dma((2, 2)), dma((4,)),
        dma((4,)), dma((4,)),
    ]
    return pl.pallas_call(
        kernel,
        out_shape=jax.ShapeDtypeStruct((half, cw), F32),
        in_specs=[anywhere, anywhere, vmem, vmem, vmem, vmem, vmem, anywhere, anywhere],
        out_specs=vmem,
        scratch_shapes=scratch,
        compiler_params=pltpu.CompilerParams(
            collective_id=0, has_side_effects=True, vmem_limit_bytes=48 * 1024 * 1024
        ),
    )(tokens, targets, expert_ids, gate_weights, gate_proj, up_proj, down_global, first, second)


def on_device(
    tokens,
    targets,
    expert_ids,
    gate_weights,
    gate_proj,
    up_proj,
    down_global,
    outer_momentum,
    inner_first,
    inner_second,
):
    islands = lax.axis_size("island")
    chunk = down_global.shape[1]
    packed = summed_steps(
        tokens[0], targets[0], expert_ids[0], gate_weights[0],
        gate_proj, up_proj, down_global, inner_first[0], inner_second[0],
    )
    total = jnp.concatenate([packed[:, :chunk], packed[:, chunk:]], axis=0)
    mean = inner_rate * (total / islands + decay_rate * down_global)
    new_momentum = outer_mu * outer_momentum + mean
    new_down = down_global - outer_rate * (mean + outer_mu * new_momentum)
    return (new_down, new_momentum)


def solution(mesh):
    return jax.shard_map(
        on_device,
        mesh=mesh,
        in_specs=(
            P(None, ("island", "expert"), None),
            P(None, ("island", "expert"), None),
            P(None, ("island", "expert"), None),
            P(None, ("island", "expert"), None),
            P("expert", "island"),
            P("expert", "island"),
            P("expert", "island"),
            P("expert", "island"),
            P("island", "expert", None),
            P("island", "expert", None),
        ),
        out_specs=(P("expert", "island"), P("expert", "island")),
        check_vma=False,
    )
```

time: 603 us -> 114 us (0.19)
  the two profiles are of different devices: /device:TPU:1 before, /device:TPU:9 now
where the time goes in v1:
time: 114 us
  Pallas kernels  103 us (90%)
  local copies, waits for them, and re-layouts  9.37 us (8%)
    pallas_call x1, Pallas kernels, summed_steps(): pl.pallas_call(kernel, out_shape=jax.ShapeDtypeStruct((half, cw), F32), i...  103 us
    unnamed x18, local copies, waits for them, and re-layouts  9.29 us

profile of v1, /device:TPU:9, one launch (start us, length us, event | category | flops | bytes accessed | tf_op | source)
XLA Modules:
  0.0 113.6 jit_solution(1351730873320461423)
XLA Ops:
  0.6 0.8 copy.12
  1.4 0.8 copy.13
  2.2 0.0 copy-start
  2.2 1.3 %copy-done = bf16[1,128,5120]{2,1,0:T(8,128)(2,1)S(1)} copy-done((bf16[1,128,5120]{2,1,0:T(8,128)(2,1)S(1)}, bf16[1,128,5120]{2,1,0:T(8,128)(2,1)}, u32[]{:S(2)}) %copy-start) | copy-done | bytes 1310744
  3.5 0.0 copy-start.1
  3.5 1.3 %copy-done.1 = bf16[1,128,5120]{2,1,0:T(8,128)(2,1)S(1)} copy-done((bf16[1,128,5120]{2,1,0:T(8,128)(2,1)S(1)}, bf16[1,128,5120]{2,1,0:T(8,128)(2,1)}, u32[]{:S(2)}) %copy-start.1) | copy-done | bytes 1310744
  4.8 0.0 copy-start.2
  4.8 1.2 %copy-done.2 = bf16[1,96,5120]{2,1,0:T(8,128)(2,1)S(1)} copy-done((bf16[1,96,5120]{2,1,0:T(8,128)(2,1)S(1)}, bf16[1,96,5120]{2,1,0:T(8,128)(2,1)}, u32[]{:S(2)}) %copy-start.2) | copy-done | bytes 983064
  6.0 0.0 copy-start.3
  6.0 1.2 %copy-done.3 = bf16[1,96,5120]{2,1,0:T(8,128)(2,1)S(1)} copy-done((bf16[1,96,5120]{2,1,0:T(8,128)(2,1)S(1)}, bf16[1,96,5120]{2,1,0:T(8,128)(2,1)}, u32[]{:S(2)}) %copy-start.3) | copy-done | bytes 983064
  7.2 0.0 copy-start.4
  7.3 0.9 copy-done.4
  8.2 0.0 copy-start.5
  8.2 0.9 copy-done.5
  9.0 0.0 copy-start.6
  9.0 0.9 copy-done.6
  9.9 0.0 copy-start.7
  9.9 102.8 %shard_map.113 = f32[48,640]{1,0:T(8,128)S(1)} custom-call(bf16[128,5120]{1,0:T(8,128)(2,1)S(1)} %bitcast.6, bf16[128,5120]{1,0:T(8,128)(2,1)S(1)} %bitcast.7, s32[128,6]{1,0:T(8,128)S(1)} %bitcast.10, f32[128,6]{1,0:T(8,128)S(1)} %bitcast.11, bf16[96,320]{1,0:T(8,128)(2,1)S(1)} %copy-done.5, bf16[96,320]{1,0:T(8,128)(2,1)S(1)} %copy-done.6, ...), custom_call_target="tpu_custom_call" | custom-call | tf_op jit(solution)/shard_map/pallas_call | solution.py:418
  112.7 0.1 fusion.2
  112.8 0.0 copy-done.7
  112.8 0.8 multiply_subtract_fusion
Async XLA Ops:
  2.2 1.3 %copy-start = (bf16[1,128,5120]{2,1,0:T(8,128)(2,1)S(1)}, bf16[1,128,5120]{2,1,0:T(8,128)(2,1)}, u32[]{:S(2)}) copy-start(bf16[1,128,5120]{2,1,0:T(8,128)(2,1)} %param.10) | copy-start | bytes 3932164
  3.5 1.3 %copy-start.1 = (bf16[1,128,5120]{2,1,0:T(8,128)(2,1)S(1)}, bf16[1,128,5120]{2,1,0:T(8,128)(2,1)}, u32[]{:S(2)}) copy-start(bf16[1,128,5120]{2,1,0:T(8,128)(2,1)} %param.11) | copy-start | bytes 3932164
  4.8 1.2 %copy-start.2 = (bf16[1,96,5120]{2,1,0:T(8,128)(2,1)S(1)}, bf16[1,96,5120]{2,1,0:T(8,128)(2,1)}, u32[]{:S(2)}) copy-start(bf16[1,96,5120]{2,1,0:T(8,128)(2,1)} %param.18) | copy-start | bytes 2949124
  6.0 1.2 %copy-start.3 = (bf16[1,96,5120]{2,1,0:T(8,128)(2,1)S(1)}, bf16[1,96,5120]{2,1,0:T(8,128)(2,1)}, u32[]{:S(2)}) copy-start(bf16[1,96,5120]{2,1,0:T(8,128)(2,1)} %param.19) | copy-start | bytes 2949124
  7.2 0.9 copy-start.4
  8.2 0.9 copy-start.5
  9.0 0.9 copy-start.6
  9.9 102.9 %copy-start.7 = (f32[96,320]{1,0:T(8,128)S(1)}, f32[96,320]{1,0:T(8,128)}, u32[]{:S(2)}) copy-start(f32[96,320]{1,0:T(8,128)} %param.17) | copy-start | bytes 368644

commit v2 on v1

v2 whole, which is shorter than its diff:
```python
import jax
import jax.numpy as jnp
from jax import lax
from jax.experimental import pallas as pl
from jax.experimental.pallas import tpu as pltpu
from jax.sharding import PartitionSpec as P

CAP = 8
SLOT = 2 * CAP
LANES = 128

beta_first = 0.9
beta_second = 0.95
inner_rate = 0.01
decay_rate = 0.1
epsilon = 1e-08
outer_rate = 0.7
outer_mu = 0.9

F32 = jnp.float32
BF16 = jnp.bfloat16
MESH = pl.DeviceIdType.MESH
ROWS_T = (((0,), (0,)), ((), ()))
COLS_T = (((1,), (1,)), ((), ()))


def wait_for(ref, sem):
    pltpu.make_async_copy(ref, ref, sem).wait()


def loop(low, high, body):
    lax.fori_loop(low, high, lambda i, _: (body(i), 0)[1], 0)


def kernel(
    tok_hbm, tgt_hbm, ids_hbm, gw_hbm, gate_hbm, up_hbm, down_hbm, m_hbm, v_hbm,
    out_ref,
    ids_ref, gw_ref, gate_ref, up_ref, down_ref, tok, tgt, sel, sbuf, xyb, xs, xp, ys, gs, lhs,
    gut, dt, gu, dd, dx, mv, part, pb, pr, ab, wn, eb, gr, ub, r1, st, r2,
    in_sem, gu_s, gu_r, gus1_s, d_s, d_r, ds1_s, xy_s, xy_r, xp_s, xp_r, dx_s, dx_r,
    mv_s, mv_r, p_s, p_r, a_s, a_r, u_s, u_r, t_s, t_r,
):
    isl = lax.axis_index("island")
    t = lax.axis_index("expert")
    x, yh = lax.rem(isl, 4), lax.div(isl, 4)
    e, pos = lax.div(t, 8), lax.rem(t, 8)
    c, core = lax.div(pos, 2), lax.rem(pos, 2)
    base = 8 * e
    pair = t + 1 - 2 * core
    right = yh * 4 + lax.rem(x + 1, 4)
    left = yh * 4 + lax.rem(x + 3, 4)
    hid, chunk = gate_ref.shape
    half = hid // 2
    cw = 2 * chunk
    odd = lax.rem(yh, 2)

    def lag(place):
        low = 3 - 2 * place
        high = jnp.where(place == 2, 2 * odd, 2 - 2 * odd)
        return jnp.where(place < 2, low, high)

    yh_cols = lax.rem(yh + lag(c), 4)
    home = yh_cols == yh
    away = yh_cols != yh
    place_at = (2 + odd, 0, 3 - odd, 1)
    zp, yl = lax.div(c, 2), lax.rem(c, 2)

    def flip(bit, by):
        return bit + by - 2 * bit * by

    def near(i):
        return 2 * flip(zp, lax.rem(i, 2)) + flip(yl, lax.div(i, 2))

    def send(src, dst, s, r, island, expert):
        pltpu.make_async_remote_copy(
            src_ref=src, dst_ref=dst, send_sem=s, recv_sem=r,
            device_id=(island, expert), device_id_type=MESH,
        ).start()

    loads = [
        pltpu.make_async_copy(src, dst, in_sem.at[i])
        for i, (src, dst) in enumerate((
            (gate_hbm, gate_ref), (up_hbm, up_ref), (down_hbm, down_ref), (ids_hbm, ids_ref),
            (gw_hbm, gw_ref), (tok_hbm, tok), (tgt_hbm, tgt),
        ))
    ]
    for load in loads:
        load.start()

    barrier = pltpu.get_barrier_semaphore()

    def tell(island, expert):
        pl.semaphore_signal(barrier, inc=1, device_id=(island, expert), device_id_type=MESH)

    loop(1, 32, lambda i: tell(isl, lax.rem(t + i, 32)))
    for d in range(1, 4):
        for k in range(2):
            tell(yh * 4 + lax.rem(x + d, 4), base + 2 * c + k)
        tell(lax.rem(yh + d, 4) * 4 + x, base + 2 * place_at[d] + core)

    @pl.when(away)
    def _():
        for q in range(4):
            tell(yh_cols * 4 + x, base + 2 * q + core)

    for load in loads[:2]:
        load.wait()

    row = lax.broadcasted_iota(jnp.int32, (chunk, cw), 0)
    col = lax.broadcasted_iota(jnp.int32, (chunk, cw), 1)
    put0 = (col == row).astype(F32).astype(BF16)
    put1 = (col == row + chunk).astype(F32).astype(BF16)

    def dot(a, b):
        return jnp.dot(a, b, preferred_element_type=F32)

    tile = (dot(gate_ref[...], put0) + dot(up_ref[...], put1)).astype(BF16)
    gut[0] = tile[:half]
    gut[1] = tile[half:]
    pl.semaphore_wait(barrier, jnp.where(away, 44, 40))

    def first_stage(tile, at, s):
        for d in (0, 1, 3, 2):
            expert = base + 2 * place_at[d] + core
            dst, r = at
            if d:
                send(tile, dst, s, r, lax.rem(yh + d, 4) * 4 + x, expert)
            else:

                @pl.when(away)
                def _():
                    send(tile, dst, s, r, isl, expert)

                @pl.when(jnp.logical_not(away))
                def _():
                    pltpu.make_async_copy(tile, dst, r).start()

    for h in range(2):
        first_stage(gut.at[h], (gu.at[0, c, h], gu_r.at[0, c, h]), gus1_s)
    for load in loads[2:5]:
        load.wait()
    down = down_ref[...].astype(BF16)
    dt[...] = (dot(down[:half], put0) + dot(down[half:], put1)).astype(BF16)

    n_tok = tok.shape[0]
    slot = lax.broadcasted_iota(jnp.int32, (4 * SLOT, n_tok), 0)
    named = lax.div(slot, SLOT)
    member = jnp.zeros((4 * SLOT, n_tok), F32)
    weight = jnp.zeros((1, n_tok), F32)
    for j in range(ids_ref.shape[0]):
        ids = ids_ref[j]
        member = member + (ids == named).astype(F32)
        weight = weight + jnp.where(ids < 4, gw_ref[j], 0.0)
    before = (
        lax.broadcasted_iota(jnp.int32, (n_tok, n_tok), 0)
        < lax.broadcasted_iota(jnp.int32, (n_tok, n_tok), 1)
    ).astype(F32).astype(BF16)
    rank = dot(member.astype(BF16), before)
    picked = jnp.where(rank == lax.rem(slot, CAP).astype(F32), member, 0.0)
    of_x = lax.rem(slot, SLOT) < CAP
    picked_x = jnp.where(of_x, picked, 0.0)
    sel[0] = picked_x.astype(BF16)
    sel[1] = jnp.where(of_x, 0.0, picked).astype(BF16)
    value = jnp.sum(picked_x * weight, axis=1, keepdims=True)
    high = value.astype(BF16)
    rest = value - high.astype(F32)
    mid = rest.astype(BF16)
    low = (rest - mid.astype(F32)).astype(BF16)
    glane = lax.broadcasted_iota(jnp.int32, (4 * SLOT, LANES), 1)
    gates = jnp.where(glane == 0, high.astype(F32), 0.0)
    gates = jnp.where(glane == 1, mid.astype(F32), gates)
    gates = jnp.where(glane == 2, low.astype(F32), gates).astype(BF16)

    for load in loads[5:]:
        load.wait()

    def columns_of(p):
        row = lax.rem(yh + lag(lax.div(p, 2)), 4)
        return pl.ds(pl.multiple_of((2 * row + lax.rem(p, 2)) * cw, LANES), cw)

    def dispatch(p):
        cols = columns_of(p)
        sbuf[p, :, 0:cw] = (dot(sel[0], tok[:, cols]) + dot(sel[1], tgt[:, cols])).astype(BF16)
        sbuf[p, :, cw:cw + LANES] = gates
        for j in range(4):
            block = sbuf.at[p, pl.ds(j * SLOT, SLOT)]

            @pl.when(8 * j + p != t)
            def _():
                send(block, xyb.at[t], xy_s, xy_r, isl, 8 * j + p)

            @pl.when(8 * j + p == t)
            def _():
                pltpu.make_async_copy(block, xyb.at[t], xy_r).start()

    loop(0, 8, dispatch)
    first_stage(dt, (dd.at[0, c], d_r.at[0, c]), ds1_s)

    def pass_on(buf, s, r, rel, to, island, *at):
        wait_for(buf.at[(rel, *at)], r.at[(rel, *at)])
        send(buf.at[(rel, *at)], buf.at[(to, *at)], s, r.at[(to, *at)], island, t)

    def around(buf, s, r, *h):
        def body(q):
            wait_for(buf.at[(0, q, *h)], r.at[(0, q, *h)])
            for to, island in ((3, right), (1, left)):
                send(buf.at[(0, q, *h)], buf.at[(to, q, *h)], s, r.at[(to, q, *h)], island, t)

        loop(0, 4, body)

    def forward(buf, s, r, *h):
        def body(q):
            pass_on(buf, s, r, 3, 2, right, q, *h)
            pass_on(buf, s, r, 1, 2, left, q + 2, *h)

        loop(0, 2, body)

    def others(buf, r, *h):
        def body(q):
            wait_for(buf.at[(3, q + 2, *h)], r.at[(3, q + 2, *h)])
            wait_for(buf.at[(1, q, *h)], r.at[(1, q, *h)])

        loop(0, 2, body)

    def far(buf, r, *h):
        loop(0, 4, lambda q: wait_for(buf.at[(2, q, *h)], r.at[(2, q, *h)]))

    def moments(i):
        p = 2 * near(lax.div(i, 2)) + flip(core, lax.rem(i, 2))
        cols = columns_of(p)
        for j, ref in enumerate((m_hbm, v_hbm)):

            @pl.when(i > 0)
            def _():
                send(ref.at[:, cols], mv.at[i, j], mv_s, mv_r.at[i], isl, base + p)

            @pl.when(i == 0)
            def _():
                pltpu.make_async_copy(ref.at[:, cols], mv.at[i, j], mv_r.at[i]).start()

    for h in range(2):
        around(gu, gu_s, gu_r, h)
    loop(0, 8, moments)
    for h in range(2):
        forward(gu, gu_s, gu_r, h)
    around(dd, d_s, d_r)

    in_low = lax.broadcasted_iota(jnp.int32, (8 * CAP, cw), 1) < chunk

    def spread(v, h, rows):
        turned = pltpu.roll(v, chunk, 1)
        up_rows = pl.ds(rows.start + 32 * CAP, rows.size)
        lhs[2 * h, rows] = jnp.where(in_low, v, 0.0).astype(BF16)
        lhs[2 * h, up_rows] = jnp.where(in_low, 0.0, turned).astype(BF16)
        lhs[2 * h + 1, rows] = jnp.where(in_low, turned, 0.0).astype(BF16)
        lhs[2 * h + 1, up_rows] = jnp.where(in_low, 0.0, v).astype(BF16)

    wait_for(xyb, xy_r)

    def unpack(i):
        v = xyb[pl.ds(8 * i, 8)].astype(F32)
        rows = pl.ds(pl.multiple_of(i * 8 * CAP, 8 * CAP), 8 * CAP)
        xv = v[:, :CAP, :cw].reshape(8 * CAP, cw)
        xs[rows] = xv.astype(BF16)
        ys[rows] = v[:, CAP:, :cw].reshape(8 * CAP, cw)
        total = jnp.sum(v[:, :CAP, cw:].reshape(8 * CAP, LANES), axis=1, keepdims=True)
        gs[rows] = jnp.broadcast_to(total, (8 * CAP, LANES))
        spread(xv, core, rows)

    loop(0, 4, unpack)
    send(xs, xp, xp_s, xp_r, isl, pair)
    wait_for(xp, xp_r)

    def unpack_pair(i):
        rows = pl.ds(pl.multiple_of(i * 8 * CAP, 8 * CAP), 8 * CAP)
        spread(xp[rows].astype(F32), 1 - core, rows)

    loop(0, 4, unpack_pair)

    def pre(rel):
        made = lax.dot_general(
            lhs[lax.rem(x + rel, 4)], gu[rel].reshape(4 * hid, cw), COLS_T, preferred_element_type=F32
        )
        return made.reshape(2, 4, 8 * CAP, 4 * hid)

    part[...] = pre(0)
    for h in range(2):
        others(gu, gu_r, h)
    part[...] += pre(1)
    part[...] += pre(3)
    for h in range(2):
        far(gu, gu_r, h)
    part[...] += pre(2)
    pb[...] = part[...].astype(BF16)
    for d in range(1, 4):
        q = lax.rem(c + d, 4)
        send(pb.at[:, q], pr.at[4 - d], p_s, p_r.at[4 - d], isl, base + 2 * q + core)
    forward(dd, d_s, d_r)
    for d in range(1, 4):
        wait_for(pr.at[d], p_r.at[d])
    gate_sum = part[0, c] + pr[1, 0].astype(F32) + pr[2, 0].astype(F32) + pr[3, 0].astype(F32)
    up_sum = part[1, c] + pr[1, 1].astype(F32) + pr[2, 1].astype(F32) + pr[3, 1].astype(F32)
    mine = 4 * core + c
    ab[mine] = (gate_sum * jax.nn.sigmoid(gate_sum) * up_sum).astype(BF16)
    loop(1, 8, lambda i: send(ab.at[mine], ab.at[mine], a_s, a_r, isl, base + lax.rem(pos + i, 8)))

    others(dd, d_r)
    far(dd, d_r)
    for j in range(2):
        rel = lax.rem(2 * (1 - core) + j + 4 - x, 4)
        send(dd.at[rel], dx.at[j], dx_s, dx_r.at[j], isl, pair)
    in_low_h = lax.broadcasted_iota(jnp.int32, (half, cw), 1) < chunk

    def lay(k, q, w0, w1):
        top = pl.multiple_of(q * hid, hid)
        w0, w1 = w0.astype(F32), w1.astype(F32)
        wn[k, pl.ds(top, half)] = jnp.where(in_low_h, w0, pltpu.roll(w1, chunk, 1)).astype(BF16)
        wn[k, pl.ds(top + half, half)] = jnp.where(in_low_h, pltpu.roll(w0, chunk, 1), w1).astype(BF16)

    rel0 = lax.rem(2 * core + 4 - x, 4)
    rel1 = lax.rem(2 * core + 5 - x, 4)
    loop(0, 4, lambda q: lay(core, q, dd[rel0, q], dd[rel1, q]))
    for j in range(2):
        wait_for(dx.at[j], dx_r.at[j])
    loop(0, 4, lambda q: lay(1 - core, q, dx[0, q], dx[1, q]))

    wait_for(ab.at[pl.ds(0, 7)], a_r)

    def acts(k):
        return ab[4 * k:4 * k + 4].reshape(32 * CAP, 4 * hid)

    g = gs[:, 0:1]
    output = dot(acts(0), wn[0]) + dot(acts(1), wn[1])
    eb[...] = (g * (g * output - ys[...])).astype(BF16)
    for k in range(2):
        gr[k] = lax.dot_general(acts(k), eb[...], ROWS_T, preferred_element_type=F32)

    def adam(i):
        q, k = near(lax.div(i, 2)), flip(core, lax.rem(i, 2))
        grad = gr[k, pl.ds(pl.multiple_of(q * hid, hid), hid)]
        wait_for(mv.at[i], mv_r.at[i])
        first = beta_first * mv[i, 0].astype(F32) + (1.0 - beta_first) * grad
        second = beta_second * mv[i, 1].astype(F32) + (1.0 - beta_second) * grad * grad
        step = first / (jnp.sqrt(second) + epsilon)
        upper, lower = step[:half], step[half:]
        ub[i, 0] = jnp.where(in_low_h, upper, pltpu.roll(lower, chunk, 1)).astype(BF16)
        ub[i, 1] = jnp.where(in_low_h, pltpu.roll(upper, chunk, 1), lower).astype(BF16)
        for j in range(2):
            stays = jnp.logical_and(2 * core + j == x, core == k)
            dst, r = r1.at[x, q], u_r.at[x, q]

            @pl.when(jnp.logical_not(stays))
            def _():
                send(ub.at[i, j], dst, u_s, r, yh * 4 + 2 * core + j, base + 2 * c + k)

            @pl.when(stays)
            def _():
                pltpu.make_async_copy(ub.at[i, j], dst, r).start()

    loop(0, 8, adam)

    def column(i):
        q = near(i)
        for j in range(4):
            wait_for(r1.at[j, q], u_r.at[j, q])
        total = r1[0, q].astype(F32) + r1[1, q].astype(F32) + r1[2, q].astype(F32) + r1[3, q].astype(F32)
        st[q] = total.astype(st.dtype)
        stays = jnp.logical_and(home, i == 0)

        @pl.when(jnp.logical_not(stays))
        def _():
            send(st.at[q], r2.at[yh], t_s, t_r.at[yh], yh_cols * 4 + x, base + 2 * q + core)

        @pl.when(stays)
        def _():
            pltpu.make_async_copy(st.at[q], r2.at[yh], t_r.at[yh]).start()

    loop(0, 4, column)
    loop(0, 4, lambda i: wait_for(r2.at[i], t_r.at[i]))
    out_ref[...] = r2[0].astype(F32) + r2[1].astype(F32) + r2[2].astype(F32) + r2[3].astype(F32)

    for buf, s, s1 in ((gu, gu_s, gus1_s), (dd, d_s, ds1_s)):
        wait_for(buf.at[pl.ds(0, 3)], s)

        @pl.when(away)
        def _():
            wait_for(buf.at[0], s1)

        @pl.when(home)
        def _():
            wait_for(buf.at[0, pl.ds(0, 3)], s1)

    wait_for(xyb.at[pl.ds(0, 31)], xy_s)
    wait_for(xs, xp_s)
    wait_for(dx, dx_s)
    wait_for(mv.at[pl.ds(0, 7)], mv_s)
    wait_for(pr.at[pl.ds(0, 3)], p_s)
    wait_for(ab.at[pl.ds(0, 7)], a_s)
    keeps = core == lax.div(x, 2)

    @pl.when(keeps)
    def _():
        wait_for(r1.at[pl.ds(0, 3)], u_s)

    @pl.when(jnp.logical_not(keeps))
    def _():
        wait_for(r1, u_s)

    @pl.when(home)
    def _():
        wait_for(st.at[pl.ds(0, 3)], t_s)

    @pl.when(away)
    def _():
        wait_for(st, t_s)


def summed_steps(tokens, targets, expert_ids, gate_weights, gate_proj, up_proj, down_global, first, second):
    n_tok, width = tokens.shape
    hid, chunk = gate_proj.shape
    half, cw = hid // 2, 2 * chunk
    rows = 32 * CAP
    dma = pltpu.SemaphoreType.DMA
    hbm = pl.BlockSpec(memory_space=pltpu.HBM)
    vmem = pl.BlockSpec(memory_space=pltpu.VMEM)
    scratch = [
        pltpu.VMEM(expert_ids.shape, jnp.int32),
        pltpu.VMEM(gate_weights.shape, F32),
        pltpu.VMEM((hid, chunk), BF16),
        pltpu.VMEM((hid, chunk), BF16),
        pltpu.VMEM((hid, chunk), F32),
        pltpu.VMEM((n_tok, width), BF16),
        pltpu.VMEM((n_tok, width), BF16),
        pltpu.VMEM((2, 4 * SLOT, n_tok), BF16),
        pltpu.VMEM((8, 4 * SLOT, cw + LANES), BF16),
        pltpu.VMEM((32, SLOT, cw + LANES), BF16),
        pltpu.VMEM((rows, cw), BF16),
        pltpu.VMEM((rows, cw), BF16),
        pltpu.VMEM((rows, cw), F32),
        pltpu.VMEM((rows, LANES), F32),
        pltpu.VMEM((4, 2 * rows, cw), BF16),
        pltpu.VMEM((2, half, cw), BF16),
        pltpu.VMEM((half, cw), BF16),
        pltpu.VMEM((4, 4, 2, half, cw), BF16),
        pltpu.VMEM((4, 4, half, cw), BF16),
        pltpu.VMEM((2, 4, half, cw), BF16),
        pltpu.VMEM((8, 2, hid, cw), BF16),
        pltpu.VMEM((2, 4, 8 * CAP, 4 * hid), F32),
        pltpu.VMEM((2, 4, 8 * CAP, 4 * hid), BF16),
        pltpu.VMEM((4, 2, 8 * CAP, 4 * hid), BF16),
        pltpu.VMEM((8, 8 * CAP, 4 * hid), BF16),
        pltpu.VMEM((2, 4 * hid, cw), BF16),
        pltpu.VMEM((rows, cw), BF16),
        pltpu.VMEM((2, 4 * hid, cw), F32),
        pltpu.VMEM((8, 2, half, cw), BF16),
        pltpu.VMEM((4, 4, half, cw), BF16),
        pltpu.VMEM((4, half, cw), BF16),
        pltpu.VMEM((4, half, cw), BF16),
        dma((7,)),
        dma, dma((4, 4, 2)), dma,
        dma, dma((4, 4)), dma,
        dma, dma, dma, dma,
        dma, dma((2,)),
        dma, dma((8,)),
        dma, dma((4,)),
        dma, dma,
        dma, dma((4, 4)),
        dma, dma((4,)),
    ]
    return pl.pallas_call(
        kernel,
        out_shape=jax.ShapeDtypeStruct((half, cw), F32),
        in_specs=[hbm] * 9,
        out_specs=vmem,
        scratch_shapes=scratch,
        compiler_params=pltpu.CompilerParams(
            collective_id=0, has_side_effects=True, vmem_limit_bytes=64 * 1024 * 1024
        ),
    )(tokens, targets, expert_ids, gate_weights, gate_proj, up_proj, down_global, first, second)


def on_device(
    tokens,
    targets,
    expert_ids,
    gate_weights,
    gate_proj,
    up_proj,
    down_global,
    outer_momentum,
    inner_first,
    inner_second,
):
    islands = lax.axis_size("island")
    chunk = down_global.shape[1]
    packed = summed_steps(
        tokens[0], targets[0],
        jnp.transpose(expert_ids, (2, 0, 1)), jnp.transpose(gate_weights, (2, 0, 1)),
        gate_proj, up_proj, down_global, inner_first[0], inner_second[0],
    )
    total = jnp.concatenate([packed[:, :chunk], packed[:, chunk:]], axis=0)
    mean = inner_rate * (total / islands + decay_rate * down_global)
    new_momentum = outer_mu * outer_momentum + mean
    new_down = down_global - outer_rate * (mean + outer_mu * new_momentum)
    return (new_down, new_momentum)


def solution(mesh):
    return jax.shard_map(
        on_device,
        mesh=mesh,
        in_specs=(
            P(None, ("island", "expert"), None),
            P(None, ("island", "expert"), None),
            P(None, ("island", "expert"), None),
            P(None, ("island", "expert"), None),
            P("expert", "island"),
            P("expert", "island"),
            P("expert", "island"),
            P("expert", "island"),
            P("island", "expert", None),
            P("island", "expert", None),
        ),
        out_specs=(P("expert", "island"), P("expert", "island")),
        check_vma=False,
    )
```

time: 114 us -> 99.4 us (0.87)
  the two profiles are of different devices: /device:TPU:9 before, /device:TPU:1 now
where the time goes in v2:
time: 99.4 us; the launch traced here: 99.2 us
  Pallas kernels  95.7 us (96%)
  other arithmetic  1.76 us (2%)
  local copies, waits for them, and re-layouts  1.04 us (1%)
    pallas_call x1, Pallas kernels, summed_steps(): pl.pallas_call(kernel, out_shape=jax.ShapeDtypeStruct((half, cw), F32), i...  95.7 us

profile of v2, /device:TPU:1, one launch (start us, length us, event | category | flops | bytes accessed | tf_op | source)
XLA Modules:
  0.0 99.2 jit_solution(8714515781744018237)
XLA Ops:
  0.6 95.7 %shard_map.113 = f32[48,640]{1,0:T(8,128)} custom-call(bf16[128,5120]{1,0:T(8,128)(2,1)} %bitcast.6, bf16[128,5120]{1,0:T(8,128)(2,1)} %bitcast.7, s32[6,1,128]{2,1,0:T(1,128)} %bitcast.10, f32[6,1,128]{2,1,0:T(1,128)} %bitcast.11, bf16[96,320]{1,0:T(8,128)(2,1)} %gate_hbm.1, bf16[96,320]{1,0:T(8,128)(2,1)} %up_hbm.1, f32[96,320]{1,0:T(8,128)} %down_hbm.1, ...), custom_call_target="tpu_custom_call" | custom-call | tf_op jit(solution)/shard_map/pallas_call | solution.py:470
  96.4 1.0 %fusion.2 = (f32[48,320]{1,0:T(8,128)S(1)}, f32[48,320]{1,0:T(8,128)S(1)}) fusion(f32[48,640]{1,0:T(8,128)} %shard_map.113), kind=kLoop, calls=%fused_computation.5 | loop fusion | bytes 245760 | tf_op jit(solution)/shard_map/slice | solution.py:501
  97.4 1.8 %multiply_subtract_fusion = (f32[96,320]{1,0:T(8,128)}, f32[96,320]{1,0:T(8,128)}) fusion(f32[96,320]{1,0:T(8,128)} %down_hbm.1, f32[48,320]{1,0:T(8,128)S(1)} %get-tuple-element.5, f32[48,320]{1,0:T(8,128)S(1)} %get-tuple-element.4, f32[96,320]{1,0:T(8,128)} %param.17), kind=kLoop, calls=%fused_computation.3 | loop fusion | flops 337920 | bytes 614400 | tf_op jit(solution)/shard_map/sub | solution.py:504

commit v3 on v2

--- a/solution.py
+++ b/solution.py
@@ -35,10 +35,10 @@
 def kernel(
     tok_hbm, tgt_hbm, ids_hbm, gw_hbm, gate_hbm, up_hbm, down_hbm, m_hbm, v_hbm,
     out_ref,
-    ids_ref, gw_ref, gate_ref, up_ref, down_ref, tok, tgt, sel, sbuf, xyb, xs, xp, ys, gs, lhs,
-    gut, dt, gu, dd, dx, mv, part, pb, pr, ab, wn, eb, gr, ub, r1, st, r2,
-    in_sem, gu_s, gu_r, gus1_s, d_s, d_r, ds1_s, xy_s, xy_r, xp_s, xp_r, dx_s, dx_r,
-    mv_s, mv_r, p_s, p_r, a_s, a_r, u_s, u_r, t_s, t_r,
+    ids_ref, gw_ref, gate_ref, up_ref, down_ref, tok, tgt, sel, grow, gbuf, sbuf, xyb, xs, xp, ys, gs, lhs,
+    gut, dt, gu, dd, dx, mv, part, pb, pr, ab, wn, eb, own, gr, ub, r1, st, r2,
+    in_sem, gu_s, gu_r, gus1_s, d_s, d_r, ds1_s, xy_s, xy_r, g_s, g_r, xp_s, xp_r, dx_s, dx_r,
+    mv_s, mv_r, p_s, p_r, a_s, a_r, e_s, e_r, u_s, u_r, t_s, t_r,
 ):
     isl = lax.axis_index("island")
     t = lax.axis_index("expert")
@@ -68,8 +68,11 @@
     def flip(bit, by):
         return bit + by - 2 * bit * by
 
+    def beside(dz, dy):
+        return 2 * flip(zp, dz) + flip(yl, dy)
+
     def near(i):
-        return 2 * flip(zp, lax.rem(i, 2)) + flip(yl, lax.div(i, 2))
+        return beside(lax.rem(i, 2), lax.div(i, 2))
 
     def send(src, dst, s, r, island, expert):
         pltpu.make_async_remote_copy(
@@ -97,6 +100,7 @@
         for k in range(2):
             tell(yh * 4 + lax.rem(x + d, 4), base + 2 * c + k)
         tell(lax.rem(yh + d, 4) * 4 + x, base + 2 * place_at[d] + core)
+        tell(lax.rem(yh + d, 4) * 4 + x, t)
 
     @pl.when(away)
     def _():
@@ -117,7 +121,7 @@
     tile = (dot(gate_ref[...], put0) + dot(up_ref[...], put1)).astype(BF16)
     gut[0] = tile[:half]
     gut[1] = tile[half:]
-    pl.semaphore_wait(barrier, jnp.where(away, 44, 40))
+    pl.semaphore_wait(barrier, jnp.where(away, 47, 43))
 
     def first_stage(tile, at, s):
         for d in (0, 1, 3, 2):
@@ -161,15 +165,17 @@
     picked_x = jnp.where(of_x, picked, 0.0)
     sel[0] = picked_x.astype(BF16)
     sel[1] = jnp.where(of_x, 0.0, picked).astype(BF16)
-    value = jnp.sum(picked_x * weight, axis=1, keepdims=True)
-    high = value.astype(BF16)
-    rest = value - high.astype(F32)
+    high = weight.astype(BF16)
+    rest = weight - high.astype(F32)
     mid = rest.astype(BF16)
     low = (rest - mid.astype(F32)).astype(BF16)
-    glane = lax.broadcasted_iota(jnp.int32, (4 * SLOT, LANES), 1)
-    gates = jnp.where(glane == 0, high.astype(F32), 0.0)
-    gates = jnp.where(glane == 1, mid.astype(F32), gates)
-    gates = jnp.where(glane == 2, low.astype(F32), gates).astype(BF16)
+    layer = lax.broadcasted_iota(jnp.int32, (8, n_tok), 0)
+    three = jnp.where(layer == 0, high.astype(F32), 0.0)
+    three = jnp.where(layer == 1, mid.astype(F32), three)
+    three = jnp.where(layer == 2, low.astype(F32), three).astype(BF16)
+    split = lax.dot_general(three, sel[0], COLS_T, preferred_element_type=F32)
+    grow[...] = jnp.zeros(grow.shape, F32)
+    grow[:, 0:4 * SLOT] = split[0:1] + split[1:2] + split[2:3]
 
     for load in loads[5:]:
         load.wait()
@@ -180,18 +186,19 @@
 
     def dispatch(p):
         cols = columns_of(p)
-        sbuf[p, :, 0:cw] = (dot(sel[0], tok[:, cols]) + dot(sel[1], tgt[:, cols])).astype(BF16)
-        sbuf[p, :, cw:cw + LANES] = gates
+        sbuf[p] = (dot(sel[0], tok[:, cols]) + dot(sel[1], tgt[:, cols])).astype(BF16)
         for j in range(4):
             block = sbuf.at[p, pl.ds(j * SLOT, SLOT)]
 
             @pl.when(8 * j + p != t)
             def _():
                 send(block, xyb.at[t], xy_s, xy_r, isl, 8 * j + p)
+                send(grow, gbuf.at[t], g_s, g_r, isl, 8 * j + p)
 
             @pl.when(8 * j + p == t)
             def _():
                 pltpu.make_async_copy(block, xyb.at[t], xy_r).start()
+                pltpu.make_async_copy(grow, gbuf.at[t], g_r).start()
 
     loop(0, 8, dispatch)
     first_stage(dt, (dd.at[0, c], d_r.at[0, c]), ds1_s)
@@ -226,21 +233,14 @@
         loop(0, 4, lambda q: wait_for(buf.at[(2, q, *h)], r.at[(2, q, *h)]))
 
     def moments(i):
-        p = 2 * near(lax.div(i, 2)) + flip(core, lax.rem(i, 2))
-        cols = columns_of(p)
+        here, there = columns_of(2 * near(i) + core), columns_of(2 * near(i) + 1 - core)
         for j, ref in enumerate((m_hbm, v_hbm)):
-
-            @pl.when(i > 0)
-            def _():
-                send(ref.at[:, cols], mv.at[i, j], mv_s, mv_r.at[i], isl, base + p)
-
-            @pl.when(i == 0)
-            def _():
-                pltpu.make_async_copy(ref.at[:, cols], mv.at[i, j], mv_r.at[i]).start()
+            pltpu.make_async_copy(ref.at[:, here], mv.at[i, 0, j], mv_r.at[0]).start()
+            send(ref.at[:, there], mv.at[i, 1, j], mv_s, mv_r.at[1], isl, pair)
 
     for h in range(2):
         around(gu, gu_s, gu_r, h)
-    loop(0, 8, moments)
+    loop(0, 4, moments)
     for h in range(2):
         forward(gu, gu_s, gu_r, h)
     around(dd, d_s, d_r)
@@ -256,14 +256,20 @@
         lhs[2 * h + 1, up_rows] = jnp.where(in_low, 0.0, v).astype(BF16)
 
     wait_for(xyb, xy_r)
+    wait_for(gbuf, g_r)
+
+    is_own = lax.broadcasted_iota(jnp.int32, (8 * CAP, LANES), 1) == SLOT * e + lax.rem(
+        lax.broadcasted_iota(jnp.int32, (8 * CAP, LANES), 0), CAP
+    )
 
     def unpack(i):
         v = xyb[pl.ds(8 * i, 8)].astype(F32)
         rows = pl.ds(pl.multiple_of(i * 8 * CAP, 8 * CAP), 8 * CAP)
-        xv = v[:, :CAP, :cw].reshape(8 * CAP, cw)
+        xv = v[:, :CAP].reshape(8 * CAP, cw)
         xs[rows] = xv.astype(BF16)
-        ys[rows] = v[:, CAP:, :cw].reshape(8 * CAP, cw)
-        total = jnp.sum(v[:, :CAP, cw:].reshape(8 * CAP, LANES), axis=1, keepdims=True)
+        ys[rows] = v[:, CAP:].reshape(8 * CAP, cw)
+        every = jnp.broadcast_to(gbuf[pl.ds(8 * i, 8)], (8, CAP, LANES)).reshape(8 * CAP, LANES)
+        total = jnp.sum(jnp.where(is_own, every, 0.0), axis=1, keepdims=True)
         gs[rows] = jnp.broadcast_to(total, (8 * CAP, LANES))
         spread(xv, core, rows)
 
@@ -331,51 +337,72 @@
 
     g = gs[:, 0:1]
     output = dot(acts(0), wn[0]) + dot(acts(1), wn[1])
-    eb[...] = (g * (g * output - ys[...])).astype(BF16)
-    for k in range(2):
-        gr[k] = lax.dot_general(acts(k), eb[...], ROWS_T, preferred_element_type=F32)
-
-    def adam(i):
-        q, k = near(lax.div(i, 2)), flip(core, lax.rem(i, 2))
-        grad = gr[k, pl.ds(pl.multiple_of(q * hid, hid), hid)]
-        wait_for(mv.at[i], mv_r.at[i])
-        first = beta_first * mv[i, 0].astype(F32) + (1.0 - beta_first) * grad
-        second = beta_second * mv[i, 1].astype(F32) + (1.0 - beta_second) * grad * grad
-        step = first / (jnp.sqrt(second) + epsilon)
-        upper, lower = step[:half], step[half:]
-        ub[i, 0] = jnp.where(in_low_h, upper, pltpu.roll(lower, chunk, 1)).astype(BF16)
-        ub[i, 1] = jnp.where(in_low_h, pltpu.roll(upper, chunk, 1), lower).astype(BF16)
-        for j in range(2):
-            stays = jnp.logical_and(2 * core + j == x, core == k)
-            dst, r = r1.at[x, q], u_r.at[x, q]
-
-            @pl.when(jnp.logical_not(stays))
-            def _():
-                send(ub.at[i, j], dst, u_s, r, yh * 4 + 2 * core + j, base + 2 * c + k)
-
-            @pl.when(stays)
-            def _():
-                pltpu.make_async_copy(ub.at[i, j], dst, r).start()
-
-    loop(0, 8, adam)
+    eb[0] = (g * (g * output - ys[...])).astype(BF16)
+    for i, (dz, dy) in ((1, (1, 0)), (2, (0, 1)), (3, (1, 1))):
+        send(eb.at[0], eb.at[i], e_s, e_r.at[i], isl, base + 2 * beside(dz, dy) + core)
+
+    unit = lax.broadcasted_iota(jnp.int32, (4 * hid, 2 * hid), 0)
+    place = lax.broadcasted_iota(jnp.int32, (4 * hid, 2 * hid), 1)
+    of_core = lax.div(place, hid)
+    want = c * hid + lax.rem(place, hid)
+    taken = [
+        dot(acts(k), jnp.logical_and(unit == want, of_core == k).astype(F32).astype(BF16)) for k in range(2)
+    ]
+    own[...] = (taken[0] + taken[1]).astype(BF16)
+    for j in range(2):
+        wait_for(mv.at[pl.ds(0, 2)], mv_r.at[j])
+
+    def step_of(i):
+        @pl.when(i > 0)
+        def _():
+            wait_for(eb.at[i], e_r.at[i])
+
+        gr[...] = lax.dot_general(own[...], eb[i], ROWS_T, preferred_element_type=F32)
+        for k in range(2):
+            grad = gr[k * hid:(k + 1) * hid]
+            side = flip(core, k)
+            first = beta_first * mv[i, side, 0].astype(F32) + (1.0 - beta_first) * grad
+            second = beta_second * mv[i, side, 1].astype(F32) + (1.0 - beta_second) * grad * grad
+            step = first / (jnp.sqrt(second) + epsilon)
+            upper, lower = step[:half], step[half:]
+            ub[i, k, 0] = jnp.where(in_low_h, upper, pltpu.roll(lower, chunk, 1)).astype(BF16)
+            ub[i, k, 1] = jnp.where(in_low_h, pltpu.roll(upper, chunk, 1), lower).astype(BF16)
+            for j in range(2):
+                stays = jnp.logical_and(2 * core + j == x, core == k)
+                dst, r = r1.at[x, i], u_r.at[x, i]
+
+                @pl.when(jnp.logical_not(stays))
+                def _():
+                    send(ub.at[i, k, j], dst, u_s, r, yh * 4 + 2 * core + j, base + 2 * c + k)
+
+                @pl.when(stays)
+                def _():
+                    pltpu.make_async_copy(ub.at[i, k, j], dst, r).start()
 
     def column(i):
-        q = near(i)
         for j in range(4):
-            wait_for(r1.at[j, q], u_r.at[j, q])
-        total = r1[0, q].astype(F32) + r1[1, q].astype(F32) + r1[2, q].astype(F32) + r1[3, q].astype(F32)
-        st[q] = total.astype(st.dtype)
-        stays = jnp.logical_and(home, i == 0)
-
-        @pl.when(jnp.logical_not(stays))
+            wait_for(r1.at[j, i], u_r.at[j, i])
+        total = r1[0, i].astype(F32) + r1[1, i].astype(F32) + r1[2, i].astype(F32) + r1[3, i].astype(F32)
+        st[i] = total.astype(st.dtype)
+        to = lax.rem(yh + lag(near(i)), 4)
+
+        @pl.when(to != yh)
         def _():
-            send(st.at[q], r2.at[yh], t_s, t_r.at[yh], yh_cols * 4 + x, base + 2 * q + core)
-
-        @pl.when(stays)
+            send(st.at[i], r2.at[yh], t_s, t_r.at[yh], to * 4 + x, t)
+
+        @pl.when(to == yh)
         def _():
-            pltpu.make_async_copy(st.at[q], r2.at[yh], t_r.at[yh]).start()
-
-    loop(0, 4, column)
+            pltpu.make_async_copy(st.at[i], r2.at[yh], t_r.at[yh]).start()
+
+    def both(i):
+        step_of(i)
+
+        @pl.when(i > 0)
+        def _():
+            column(i - 1)
+
+    loop(0, 4, both)
+    column(jnp.int32(3))
     loop(0, 4, lambda i: wait_for(r2.at[i], t_r.at[i]))
     out_ref[...] = r2[0].astype(F32) + r2[1].astype(F32) + r2[2].astype(F32) + r2[3].astype(F32)
 
@@ -391,9 +418,11 @@
             wait_for(buf.at[0, pl.ds(0, 3)], s1)
 
     wait_for(xyb.at[pl.ds(0, 31)], xy_s)
+    wait_for(gbuf.at[pl.ds(0, 31)], g_s)
+    wait_for(eb.at[pl.ds(0, 3)], e_s)
     wait_for(xs, xp_s)
     wait_for(dx, dx_s)
-    wait_for(mv.at[pl.ds(0, 7)], mv_s)
+    wait_for(mv.at[pl.ds(0, 2)], mv_s)
     wait_for(pr.at[pl.ds(0, 3)], p_s)
     wait_for(ab.at[pl.ds(0, 7)], a_s)
     keeps = core == lax.div(x, 2)
@@ -406,13 +435,7 @@
     def _():
         wait_for(r1, u_s)
 
-    @pl.when(home)
-    def _():
-        wait_for(st.at[pl.ds(0, 3)], t_s)
-
-    @pl.when(away)
-    def _():
-        wait_for(st, t_s)
+    wait_for(st.at[pl.ds(0, 3)], t_s)
 
 
 def summed_steps(tokens, targets, expert_ids, gate_weights, gate_proj, up_proj, down_global, first, second):
@@ -432,8 +455,10 @@
         pltpu.VMEM((n_tok, width), BF16),
         pltpu.VMEM((n_tok, width), BF16),
         pltpu.VMEM((2, 4 * SLOT, n_tok), BF16),
-        pltpu.VMEM((8, 4 * SLOT, cw + LANES), BF16),
-        pltpu.VMEM((32, SLOT, cw + LANES), BF16),
+        pltpu.VMEM((1, LANES), F32),
+        pltpu.VMEM((32, 1, LANES), F32),
+        pltpu.VMEM((8, 4 * SLOT, cw), BF16),
+        pltpu.VMEM((32, SLOT, cw), BF16),
         pltpu.VMEM((rows, cw), BF16),
         pltpu.VMEM((rows, cw), BF16),
         pltpu.VMEM((rows, cw), F32),
@@ -444,26 +469,28 @@
         pltpu.VMEM((4, 4, 2, half, cw), BF16),
         pltpu.VMEM((4, 4, half, cw), BF16),
         pltpu.VMEM((2, 4, half, cw), BF16),
-        pltpu.VMEM((8, 2, hid, cw), BF16),
+        pltpu.VMEM((4, 2, 2, hid, cw), BF16),
         pltpu.VMEM((2, 4, 8 * CAP, 4 * hid), F32),
         pltpu.VMEM((2, 4, 8 * CAP, 4 * hid), BF16),
         pltpu.VMEM((4, 2, 8 * CAP, 4 * hid), BF16),
         pltpu.VMEM((8, 8 * CAP, 4 * hid), BF16),
         pltpu.VMEM((2, 4 * hid, cw), BF16),
-        pltpu.VMEM((rows, cw), BF16),
-        pltpu.VMEM((2, 4 * hid, cw), F32),
-        pltpu.VMEM((8, 2, half, cw), BF16),
+        pltpu.VMEM((4, rows, cw), BF16),
+        pltpu.VMEM((rows, 2 * hid), BF16),
+        pltpu.VMEM((2 * hid, cw), F32),
+        pltpu.VMEM((4, 2, 2, half, cw), BF16),
         pltpu.VMEM((4, 4, half, cw), BF16),
         pltpu.VMEM((4, half, cw), BF16),
         pltpu.VMEM((4, half, cw), BF16),
         dma((7,)),
         dma, dma((4, 4, 2)), dma,
         dma, dma((4, 4)), dma,
-        dma, dma, dma, dma,
+        dma, dma, dma, dma, dma, dma,
         dma, dma((2,)),
-        dma, dma((8,)),
+        dma, dma((2,)),
         dma, dma((4,)),
         dma, dma,
+        dma, dma((4,)),
         dma, dma((4, 4)),
         dma, dma((4,)),
     ]

time: 99.4 us -> 92.6 us (0.932)
  Pallas kernels: 95.7 us -> 88.9 us
    pallas_call x1, Pallas kernels: 95.7 us -> 88.9 us  [summed_steps(): pl.pallas_call(kernel, out_shape=jax.ShapeDtypeStruct((half, cw), F32), i...]
where the time goes in v3:
time: 92.6 us; the launch traced here: 92.4 us
  Pallas kernels  88.9 us (96%)
  other arithmetic  1.76 us (2%)
  local copies, waits for them, and re-layouts  1.04 us (1%)
    pallas_call x1, Pallas kernels, summed_steps(): pl.pallas_call(kernel, out_shape=jax.ShapeDtypeStruct((half, cw), F32), i...  88.9 us

profile of v3, /device:TPU:1, one launch (start us, length us, event | category | flops | bytes accessed | tf_op | source)
XLA Modules:
  0.0 92.4 jit_solution(12797512414283746111)
XLA Ops:
  0.6 88.9 %shard_map.113 = f32[48,640]{1,0:T(8,128)} custom-call(bf16[128,5120]{1,0:T(8,128)(2,1)} %bitcast.6, bf16[128,5120]{1,0:T(8,128)(2,1)} %bitcast.7, s32[6,1,128]{2,1,0:T(1,128)} %bitcast.10, f32[6,1,128]{2,1,0:T(1,128)} %bitcast.11, bf16[96,320]{1,0:T(8,128)(2,1)} %gate_hbm.1, bf16[96,320]{1,0:T(8,128)(2,1)} %up_hbm.1, f32[96,320]{1,0:T(8,128)} %down_hbm.1, ...), custom_call_target="tpu_custom_call" | custom-call | tf_op jit(solution)/shard_map/pallas_call | solution.py:497
  89.6 1.0 %fusion.2 = (f32[48,320]{1,0:T(8,128)S(1)}, f32[48,320]{1,0:T(8,128)S(1)}) fusion(f32[48,640]{1,0:T(8,128)} %shard_map.113), kind=kLoop, calls=%fused_computation.5 | loop fusion | bytes 245760 | tf_op jit(solution)/shard_map/slice | solution.py:528
  90.6 1.8 %multiply_subtract_fusion = (f32[96,320]{1,0:T(8,128)}, f32[96,320]{1,0:T(8,128)}) fusion(f32[96,320]{1,0:T(8,128)} %down_hbm.1, f32[48,320]{1,0:T(8,128)S(1)} %get-tuple-element.5, f32[48,320]{1,0:T(8,128)S(1)} %get-tuple-element.4, f32[96,320]{1,0:T(8,128)} %param.17), kind=kLoop, calls=%fused_computation.3 | loop fusion | flops 337920 | bytes 614400 | tf_op jit(solution)/shard_map/sub | solution.py:531

commit v4 on v3

--- a/solution.py
+++ b/solution.py
@@ -71,8 +71,10 @@
     def beside(dz, dy):
         return 2 * flip(zp, dz) + flip(yl, dy)
 
-    def near(i):
-        return beside(lax.rem(i, 2), lax.div(i, 2))
+    diagonal = beside(1, 1)
+
+    def chip(i):
+        return beside(jnp.where(i == 2, 1, 0), jnp.where(i == 3, 1, 0))
 
     def send(src, dst, s, r, island, expert):
         pltpu.make_async_remote_copy(
@@ -232,15 +234,23 @@
     def far(buf, r, *h):
         loop(0, 4, lambda q: wait_for(buf.at[(2, q, *h)], r.at[(2, q, *h)]))
 
-    def moments(i):
-        here, there = columns_of(2 * near(i) + core), columns_of(2 * near(i) + 1 - core)
+    def moments(n):
+        i = n + jnp.where(n > 0, 1, 0)
+        here, there = columns_of(2 * chip(i) + core), columns_of(2 * chip(i) + 1 - core)
         for j, ref in enumerate((m_hbm, v_hbm)):
             pltpu.make_async_copy(ref.at[:, here], mv.at[i, 0, j], mv_r.at[0]).start()
-            send(ref.at[:, there], mv.at[i, 1, j], mv_s, mv_r.at[1], isl, pair)
+            send(ref.at[:, there], mv.at[i, 1, j], mv_s.at[0], mv_r.at[1], isl, pair)
+
+    def moments_across(k):
+        other = flip(core, k)
+        cols = columns_of(2 * diagonal + other)
+        for j, ref in enumerate((m_hbm, v_hbm)):
+            send(ref.at[:, cols], mv.at[1, k, j], mv_s.at[1], mv_r.at[2 + k], isl, base + 2 * diagonal + other)
 
     for h in range(2):
         around(gu, gu_s, gu_r, h)
-    loop(0, 4, moments)
+    loop(0, 3, moments)
+    loop(0, 2, moments_across)
     for h in range(2):
         forward(gu, gu_s, gu_r, h)
     around(dd, d_s, d_r)
@@ -338,26 +348,32 @@
     g = gs[:, 0:1]
     output = dot(acts(0), wn[0]) + dot(acts(1), wn[1])
     eb[0] = (g * (g * output - ys[...])).astype(BF16)
-    for i, (dz, dy) in ((1, (1, 0)), (2, (0, 1)), (3, (1, 1))):
-        send(eb.at[0], eb.at[i], e_s, e_r.at[i], isl, base + 2 * beside(dz, dy) + core)
+    for i, to in ((1, beside(1, 0)), (2, beside(0, 1))):
+        send(eb.at[0], eb.at[i], e_s, e_r.at[i], isl, base + 2 * to + core)
 
     unit = lax.broadcasted_iota(jnp.int32, (4 * hid, 2 * hid), 0)
     place = lax.broadcasted_iota(jnp.int32, (4 * hid, 2 * hid), 1)
     of_core = lax.div(place, hid)
-    want = c * hid + lax.rem(place, hid)
-    taken = [
-        dot(acts(k), jnp.logical_and(unit == want, of_core == k).astype(F32).astype(BF16)) for k in range(2)
-    ]
-    own[...] = (taken[0] + taken[1]).astype(BF16)
-    for j in range(2):
-        wait_for(mv.at[pl.ds(0, 2)], mv_r.at[j])
+    for i, at in ((0, c), (1, diagonal)):
+        want = at * hid + lax.rem(place, hid)
+        taken = [
+            dot(acts(k), jnp.logical_and(unit == want, of_core == k).astype(F32).astype(BF16))
+            for k in range(2)
+        ]
+        own[i] = (taken[0] + taken[1]).astype(BF16)
+    wait_for(mv.at[pl.ds(0, 3), 0], mv_r.at[0])
+    wait_for(mv.at[pl.ds(0, 3), 0], mv_r.at[1])
+    for k in range(2):
+        wait_for(mv.at[1, k], mv_r.at[2 + k])
 
     def step_of(i):
-        @pl.when(i > 0)
+        errors = jnp.maximum(i - 1, 0)
+
+        @pl.when(i > 1)
         def _():
-            wait_for(eb.at[i], e_r.at[i])
-
-        gr[...] = lax.dot_general(own[...], eb[i], ROWS_T, preferred_element_type=F32)
+            wait_for(eb.at[errors], e_r.at[errors])
+
+        gr[...] = lax.dot_general(own[jnp.where(i == 1, 1, 0)], eb[errors], ROWS_T, preferred_element_type=F32)
         for k in range(2):
             grad = gr[k * hid:(k + 1) * hid]
             side = flip(core, k)
@@ -384,13 +400,15 @@
             wait_for(r1.at[j, i], u_r.at[j, i])
         total = r1[0, i].astype(F32) + r1[1, i].astype(F32) + r1[2, i].astype(F32) + r1[3, i].astype(F32)
         st[i] = total.astype(st.dtype)
-        to = lax.rem(yh + lag(near(i)), 4)
-
-        @pl.when(to != yh)
+        to = lax.rem(yh + lag(chip(i)), 4)
+        stays = jnp.logical_and(to == yh, i != 1)
+
+        @pl.when(jnp.logical_not(stays))
         def _():
-            send(st.at[i], r2.at[yh], t_s, t_r.at[yh], to * 4 + x, t)
-
-        @pl.when(to == yh)
+            expert = jnp.where(i == 1, base + 2 * diagonal + core, t)
+            send(st.at[i], r2.at[yh], t_s, t_r.at[yh], to * 4 + x, expert)
+
+        @pl.when(stays)
         def _():
             pltpu.make_async_copy(st.at[i], r2.at[yh], t_r.at[yh]).start()
 
@@ -419,10 +437,11 @@
 
     wait_for(xyb.at[pl.ds(0, 31)], xy_s)
     wait_for(gbuf.at[pl.ds(0, 31)], g_s)
-    wait_for(eb.at[pl.ds(0, 3)], e_s)
+    wait_for(eb.at[pl.ds(0, 2)], e_s)
     wait_for(xs, xp_s)
     wait_for(dx, dx_s)
-    wait_for(mv.at[pl.ds(0, 2)], mv_s)
+    wait_for(mv.at[pl.ds(0, 3), 0], mv_s.at[0])
+    wait_for(mv.at[0], mv_s.at[1])
     wait_for(pr.at[pl.ds(0, 3)], p_s)
     wait_for(ab.at[pl.ds(0, 7)], a_s)
     keeps = core == lax.div(x, 2)
@@ -435,7 +454,13 @@
     def _():
         wait_for(r1, u_s)
 
-    wait_for(st.at[pl.ds(0, 3)], t_s)
+    @pl.when(lag(diagonal) == 0)
+    def _():
+        wait_for(st, t_s)
+
+    @pl.when(lag(diagonal) != 0)
+    def _():
+        wait_for(st.at[pl.ds(0, 3)], t_s)
 
 
 def summed_steps(tokens, targets, expert_ids, gate_weights, gate_proj, up_proj, down_global, first, second):
@@ -475,8 +500,8 @@
         pltpu.VMEM((4, 2, 8 * CAP, 4 * hid), BF16),
         pltpu.VMEM((8, 8 * CAP, 4 * hid), BF16),
         pltpu.VMEM((2, 4 * hid, cw), BF16),
-        pltpu.VMEM((4, rows, cw), BF16),
-        pltpu.VMEM((rows, 2 * hid), BF16),
+        pltpu.VMEM((3, rows, cw), BF16),
+        pltpu.VMEM((2, rows, 2 * hid), BF16),
         pltpu.VMEM((2 * hid, cw), F32),
         pltpu.VMEM((4, 2, 2, half, cw), BF16),
         pltpu.VMEM((4, 4, half, cw), BF16),
@@ -487,10 +512,10 @@
         dma, dma((4, 4)), dma,
         dma, dma, dma, dma, dma, dma,
         dma, dma((2,)),
-        dma, dma((2,)),
+        dma((2,)), dma((4,)),
         dma, dma((4,)),
         dma, dma,
-        dma, dma((4,)),
+        dma, dma((3,)),
         dma, dma((4, 4)),
         dma, dma((4,)),
     ]

time: 92.6 us -> 95 us (1.026)
  Pallas kernels: 88.9 us -> 91.3 us
    pallas_call x1, Pallas kernels: 88.9 us -> 91.3 us  [summed_steps(): pl.pallas_call(kernel, out_shape=jax.ShapeDtypeStruct((half, cw), F32), i...]
where the time goes in v4:
time: 95 us; the launch traced here: 94.7 us
  Pallas kernels  91.3 us (96%)
  other arithmetic  1.76 us (2%)
  local copies, waits for them, and re-layouts  1.04 us (1%)
    pallas_call x1, Pallas kernels, summed_steps(): pl.pallas_call(kernel, out_shape=jax.ShapeDtypeStruct((half, cw), F32), i...  91.3 us

profile of v4, /device:TPU:1, one launch (start us, length us, event | category | flops | bytes accessed | tf_op | source)
XLA Modules:
  0.0 94.7 jit_solution(14004812616327471254)
XLA Ops:
  0.6 91.3 %shard_map.113 = f32[48,640]{1,0:T(8,128)} custom-call(bf16[128,5120]{1,0:T(8,128)(2,1)} %bitcast.6, bf16[128,5120]{1,0:T(8,128)(2,1)} %bitcast.7, s32[6,1,128]{2,1,0:T(1,128)} %bitcast.10, f32[6,1,128]{2,1,0:T(1,128)} %bitcast.11, bf16[96,320]{1,0:T(8,128)(2,1)} %gate_hbm.1, bf16[96,320]{1,0:T(8,128)(2,1)} %up_hbm.1, f32[96,320]{1,0:T(8,128)} %down_hbm.1, ...), custom_call_target="tpu_custom_call" | custom-call | tf_op jit(solution)/shard_map/pallas_call | solution.py:522
  91.9 1.0 %fusion.2 = (f32[48,320]{1,0:T(8,128)S(1)}, f32[48,320]{1,0:T(8,128)S(1)}) fusion(f32[48,640]{1,0:T(8,128)} %shard_map.113), kind=kLoop, calls=%fused_computation.5 | loop fusion | bytes 245760 | tf_op jit(solution)/shard_map/slice | solution.py:553
  92.9 1.8 %multiply_subtract_fusion = (f32[96,320]{1,0:T(8,128)}, f32[96,320]{1,0:T(8,128)}) fusion(f32[96,320]{1,0:T(8,128)} %down_hbm.1, f32[48,320]{1,0:T(8,128)S(1)} %get-tuple-element.5, f32[48,320]{1,0:T(8,128)S(1)} %get-tuple-element.4, f32[96,320]{1,0:T(8,128)} %param.17), kind=kLoop, calls=%fused_computation.3 | loop fusion | flops 337920 | bytes 614400 | tf_op jit(solution)/shard_map/sub | solution.py:556

commit v5 on v3

--- a/solution.py
+++ b/solution.py
@@ -267,10 +267,10 @@
         rows = pl.ds(pl.multiple_of(i * 8 * CAP, 8 * CAP), 8 * CAP)
         xv = v[:, :CAP].reshape(8 * CAP, cw)
         xs[rows] = xv.astype(BF16)
-        ys[rows] = v[:, CAP:].reshape(8 * CAP, cw)
+        ys[i] = v[:, CAP:].reshape(8 * CAP, cw)
         every = jnp.broadcast_to(gbuf[pl.ds(8 * i, 8)], (8, CAP, LANES)).reshape(8 * CAP, LANES)
         total = jnp.sum(jnp.where(is_own, every, 0.0), axis=1, keepdims=True)
-        gs[rows] = jnp.broadcast_to(total, (8 * CAP, LANES))
+        gs[i] = jnp.broadcast_to(total, (8 * CAP, LANES))
         spread(xv, core, rows)
 
     loop(0, 4, unpack)
@@ -298,17 +298,30 @@
         far(gu, gu_r, h)
     part[...] += pre(2)
     pb[...] = part[...].astype(BF16)
-    for d in range(1, 4):
-        q = lax.rem(c + d, 4)
-        send(pb.at[:, q], pr.at[4 - d], p_s, p_r.at[4 - d], isl, base + 2 * q + core)
+    part_rows = 4 * CAP
+    for h in range(2):
+        rows = pl.ds(h * part_rows, part_rows)
+        for d in range(1, 4):
+            q = lax.rem(c + d, 4)
+            to = base + 2 * q + core
+            send(pb.at[:, q, rows], pr.at[4 - d, :, rows], p_s, p_r.at[4 - d, h], isl, to)
     forward(dd, d_s, d_r)
-    for d in range(1, 4):
-        wait_for(pr.at[d], p_r.at[d])
-    gate_sum = part[0, c] + pr[1, 0].astype(F32) + pr[2, 0].astype(F32) + pr[3, 0].astype(F32)
-    up_sum = part[1, c] + pr[1, 1].astype(F32) + pr[2, 1].astype(F32) + pr[3, 1].astype(F32)
     mine = 4 * core + c
-    ab[mine] = (gate_sum * jax.nn.sigmoid(gate_sum) * up_sum).astype(BF16)
-    loop(1, 8, lambda i: send(ab.at[mine], ab.at[mine], a_s, a_r, isl, base + lax.rem(pos + i, 8)))
+
+    def activate(h):
+        rows = pl.ds(h * part_rows, part_rows)
+        for d in range(1, 4):
+            wait_for(pr.at[d, :, rows], p_r.at[d, h])
+        gate_sum, up_sum = (
+            part[j, c, rows] + pr[1, j, rows].astype(F32) + pr[2, j, rows].astype(F32) + pr[3, j, rows].astype(F32)
+            for j in range(2)
+        )
+        ab[mine, rows] = (gate_sum * jax.nn.sigmoid(gate_sum) * up_sum).astype(BF16)
+        block = ab.at[mine, rows]
+        loop(1, 8, lambda i: send(block, block, a_s, a_r.at[h], isl, base + lax.rem(pos + i, 8)))
+
+    for h in range(2):
+        activate(h)
 
     others(dd, d_r)
     far(dd, d_r)
@@ -330,25 +343,26 @@
         wait_for(dx.at[j], dx_r.at[j])
     loop(0, 4, lambda q: lay(1 - core, q, dx[0, q], dx[1, q]))
 
-    wait_for(ab.at[pl.ds(0, 7)], a_r)
-
-    def acts(k):
-        return ab[4 * k:4 * k + 4].reshape(32 * CAP, 4 * hid)
-
-    g = gs[:, 0:1]
-    output = dot(acts(0), wn[0]) + dot(acts(1), wn[1])
-    eb[0] = (g * (g * output - ys[...])).astype(BF16)
-    for i, (dz, dy) in ((1, (1, 0)), (2, (0, 1)), (3, (1, 1))):
-        send(eb.at[0], eb.at[i], e_s, e_r.at[i], isl, base + 2 * beside(dz, dy) + core)
-
+    half_rows = 4 * part_rows
     unit = lax.broadcasted_iota(jnp.int32, (4 * hid, 2 * hid), 0)
     place = lax.broadcasted_iota(jnp.int32, (4 * hid, 2 * hid), 1)
     of_core = lax.div(place, hid)
     want = c * hid + lax.rem(place, hid)
-    taken = [
-        dot(acts(k), jnp.logical_and(unit == want, of_core == k).astype(F32).astype(BF16)) for k in range(2)
-    ]
-    own[...] = (taken[0] + taken[1]).astype(BF16)
+    takes = [jnp.logical_and(unit == want, of_core == k).astype(F32).astype(BF16) for k in range(2)]
+
+    for h in range(2):
+        some = slice(h * part_rows, (h + 1) * part_rows)
+        rows = pl.ds(h * half_rows, half_rows)
+        wait_for(ab.at[pl.ds(0, 7), pl.ds(0, part_rows)], a_r.at[h])
+        acts = [ab[4 * k:4 * k + 4, some].reshape(half_rows, 4 * hid) for k in range(2)]
+        g = gs[:, some, 0:1].reshape(half_rows, 1)
+        output = dot(acts[0], wn[0]) + dot(acts[1], wn[1])
+        eb[0, rows] = (g * (g * output - ys[:, some].reshape(half_rows, cw))).astype(BF16)
+        for i, (dz, dy) in ((1, (1, 0)), (2, (0, 1)), (3, (1, 1))):
+            expert = base + 2 * beside(dz, dy) + core
+            send(eb.at[0, rows], eb.at[i, rows], e_s, e_r.at[i], isl, expert)
+        own[rows] = (dot(acts[0], takes[0]) + dot(acts[1], takes[1])).astype(BF16)
+
     for j in range(2):
         wait_for(mv.at[pl.ds(0, 2)], mv_r.at[j])
 
@@ -461,8 +475,8 @@
         pltpu.VMEM((32, SLOT, cw), BF16),
         pltpu.VMEM((rows, cw), BF16),
         pltpu.VMEM((rows, cw), BF16),
-        pltpu.VMEM((rows, cw), F32),
-        pltpu.VMEM((rows, LANES), F32),
+        pltpu.VMEM((4, 8 * CAP, cw), F32),
+        pltpu.VMEM((4, 8 * CAP, LANES), F32),
         pltpu.VMEM((4, 2 * rows, cw), BF16),
         pltpu.VMEM((2, half, cw), BF16),
         pltpu.VMEM((half, cw), BF16),
@@ -488,8 +502,8 @@
         dma, dma, dma, dma, dma, dma,
         dma, dma((2,)),
         dma, dma((2,)),
-        dma, dma((4,)),
-        dma, dma,
+        dma, dma((4, 2)),
+        dma, dma((2,)),
         dma, dma((4,)),
         dma, dma((4, 4)),
         dma, dma((4,)),

time: 92.6 us -> 89 us (0.961)
  Pallas kernels: 88.9 us -> 85.3 us
    pallas_call x1, Pallas kernels: 88.9 us -> 85.3 us  [summed_steps(): pl.pallas_call(kernel, out_shape=jax.ShapeDtypeStruct((half, cw), F32), i...]
where the time goes in v5:
time: 89 us; the launch traced here: 88.8 us
  Pallas kernels  85.3 us (96%)
  other arithmetic  1.76 us (2%)
  local copies, waits for them, and re-layouts  1.04 us (1%)
    pallas_call x1, Pallas kernels, summed_steps(): pl.pallas_call(kernel, out_shape=jax.ShapeDtypeStruct((half, cw), F32), i...  85.3 us

profile of v5, /device:TPU:1, one launch (start us, length us, event | category | flops | bytes accessed | tf_op | source)
XLA Modules:
  0.0 88.8 jit_solution(5503478475074916384)
XLA Ops:
  0.6 85.3 %shard_map.113 = f32[48,640]{1,0:T(8,128)} custom-call(bf16[128,5120]{1,0:T(8,128)(2,1)} %bitcast.6, bf16[128,5120]{1,0:T(8,128)(2,1)} %bitcast.7, s32[6,1,128]{2,1,0:T(1,128)} %bitcast.10, f32[6,1,128]{2,1,0:T(1,128)} %bitcast.11, bf16[96,320]{1,0:T(8,128)(2,1)} %gate_hbm.1, bf16[96,320]{1,0:T(8,128)(2,1)} %up_hbm.1, f32[96,320]{1,0:T(8,128)} %down_hbm.1, ...), custom_call_target="tpu_custom_call" | custom-call | tf_op jit(solution)/shard_map/pallas_call | solution.py:511
  85.9 1.0 %fusion.2 = (f32[48,320]{1,0:T(8,128)S(1)}, f32[48,320]{1,0:T(8,128)S(1)}) fusion(f32[48,640]{1,0:T(8,128)} %shard_map.113), kind=kLoop, calls=%fused_computation.5 | loop fusion | bytes 245760 | tf_op jit(solution)/shard_map/slice | solution.py:542
  87.0 1.8 %multiply_subtract_fusion = (f32[96,320]{1,0:T(8,128)}, f32[96,320]{1,0:T(8,128)}) fusion(f32[96,320]{1,0:T(8,128)} %down_hbm.1, f32[48,320]{1,0:T(8,128)S(1)} %get-tuple-element.5, f32[48,320]{1,0:T(8,128)S(1)} %get-tuple-element.4, f32[96,320]{1,0:T(8,128)} %param.17), kind=kLoop, calls=%fused_computation.3 | loop fusion | flops 337920 | bytes 614400 | tf_op jit(solution)/shard_map/sub | solution.py:545

commit v6 on v5

--- a/solution.py
+++ b/solution.py
@@ -418,7 +418,9 @@
     loop(0, 4, both)
     column(jnp.int32(3))
     loop(0, 4, lambda i: wait_for(r2.at[i], t_r.at[i]))
-    out_ref[...] = r2[0].astype(F32) + r2[1].astype(F32) + r2[2].astype(F32) + r2[3].astype(F32)
+    total = r2[0].astype(F32) + r2[1].astype(F32) + r2[2].astype(F32) + r2[3].astype(F32)
+    out_ref[0:half] = total[:, :chunk]
+    out_ref[half:hid] = pltpu.roll(total, chunk, 1)[:, :chunk]
 
     for buf, s, s1 in ((gu, gu_s, gus1_s), (dd, d_s, ds1_s)):
         wait_for(buf.at[pl.ds(0, 3)], s)
@@ -510,7 +512,7 @@
     ]
     return pl.pallas_call(
         kernel,
-        out_shape=jax.ShapeDtypeStruct((half, cw), F32),
+        out_shape=jax.ShapeDtypeStruct((hid, chunk), F32),
         in_specs=[hbm] * 9,
         out_specs=vmem,
         scratch_shapes=scratch,
@@ -533,13 +535,11 @@
     inner_second,
 ):
     islands = lax.axis_size("island")
-    chunk = down_global.shape[1]
-    packed = summed_steps(
+    total = summed_steps(
         tokens[0], targets[0],
         jnp.transpose(expert_ids, (2, 0, 1)), jnp.transpose(gate_weights, (2, 0, 1)),
         gate_proj, up_proj, down_global, inner_first[0], inner_second[0],
     )
-    total = jnp.concatenate([packed[:, :chunk], packed[:, chunk:]], axis=0)
     mean = inner_rate * (total / islands + decay_rate * down_global)
     new_momentum = outer_mu * outer_momentum + mean
     new_down = down_global - outer_rate * (mean + outer_mu * new_momentum)

time: 89 us -> 88 us (0.989)
  local copies, waits for them, and re-layouts: 1.04 us -> 0 us
    slice x1 -> x0, local copies, waits for them, and re-layouts: 1.04 us -> none  [on_device(): total = jnp.concatenate([packed[:, :chunk], packed[:, chunk:]], axis=0)]
where the time goes in v6:
time: 88 us; the launch traced here: 87.8 us
  Pallas kernels  85.4 us (97%)
  other arithmetic  1.82 us (2%)
    pallas_call x1, Pallas kernels, summed_steps(): pl.pallas_call(kernel, out_shape=jax.ShapeDtypeStruct((hid, chunk), F32),...  85.4 us
    sub x1, other arithmetic, on_device(): new_down = down_global - outer_rate * (mean + outer_mu * new_momentum)  1.82 us

profile of v6, /device:TPU:1, one launch (start us, length us, event | category | flops | bytes accessed | tf_op | source)
XLA Modules:
  0.0 87.8 jit_solution(2502583278030907700)
XLA Ops:
  0.6 85.4 %shard_map.113 = f32[96,320]{1,0:T(8,128)} custom-call(bf16[128,5120]{1,0:T(8,128)(2,1)} %bitcast.6, bf16[128,5120]{1,0:T(8,128)(2,1)} %bitcast.7, s32[6,1,128]{2,1,0:T(1,128)} %bitcast.10, f32[6,1,128]{2,1,0:T(1,128)} %bitcast.11, bf16[96,320]{1,0:T(8,128)(2,1)} %gate_hbm.1, bf16[96,320]{1,0:T(8,128)(2,1)} %up_hbm.1, f32[96,320]{1,0:T(8,128)} %down_hbm.1, ...), custom_call_target="tpu_custom_call" | custom-call | tf_op jit(solution)/shard_map/pallas_call | solution.py:513
  86.0 1.8 %multiply_subtract_fusion = (f32[96,320]{1,0:T(8,128)}, f32[96,320]{1,0:T(8,128)}) fusion(f32[96,320]{1,0:T(8,128)} %down_hbm.1, f32[96,320]{1,0:T(8,128)} %shard_map.113, f32[96,320]{1,0:T(8,128)} %param.17), kind=kLoop, calls=%fused_computation | loop fusion | flops 307200 | bytes 614400 | tf_op jit(solution)/shard_map/sub | solution.py:545
